TPU v7x, 128 devices: a whole 4x4x4 slice. The times are simulated.
128 devices in a mesh: dp: 8 (over y, x_lo), row: 16 (over z, x_hi, core).
Axes of the slice: x: 4 (x_hi: 2, x_lo: 2; x = x_hi * 2 + x_lo), y: 4, z: 4, core: 2. Of those that a mesh axis runs over, the one named last changes fastest.
Arguments:
- fields: bfloat16 [8, 128, 360, 768], P('dp', 'row'), may hold values from -6 to 6
- cotangent: bfloat16 [8, 128, 360, 768], P('dp', 'row'), may hold values from -6 to 6
- norm_gain: float32 [768], replicated, may hold values from 0.5 to 1.5
- weights: bfloat16 [2, 2, 8, 96, 96], replicated, may hold values from -0.4375 to 0.4375
- biases: float32 [2, 2, 768], replicated, may hold values from -3 to 3
- cutoffs: int32 [16], replicated, may hold values from 44 to 176, as said below
Outputs:
- block_out: bfloat16 [8, 128, 360, 768], P('dp', 'row')
- input_grad: bfloat16 [8, 128, 360, 768], P('dp', 'row')
- weight_grads: float32 [2, 2, 8, 96, 96], replicated
- bias_grads: float32 [2, 2, 768], replicated
- gain_grad: float32 [768], replicated
Inputs may be any that keep to these rules, and one draw needn't show every extreme that they name: `cutoffs`: one cutoff equals 176 and one equals 44.
All inputs are finite; a program needn't handle non-finite values.
Results may differ from a plain program's by a relative error of at most 0.015.
Values may be sent and summed in bfloat16 or wider, within the bound.
No kernel may reach another device: no remote copies, remote signals or barrier semaphores. Data moves between devices by JAX's collectives and lax.ppermute only.
A program may use at most 128 MiB of HBM per device.

v0:
```python
import math

import jax
import jax.numpy as jnp
from jax import lax
from jax.sharding import PartitionSpec as P

KW = 176


norm_eps = 1e-06
gelu_coef = 0.7978845608
cube_coef = 0.044715


def gelu_pair(values):
    inner = jnp.tanh(gelu_coef * (values + cube_coef * values * values * values))
    value = 0.5 * values * (1.0 + inner)
    slope = 0.5 * (1.0 + inner) + 0.5 * values * (1.0 - inner * inner) * gelu_coef * (
        1.0 + 3.0 * cube_coef * values * values
    )
    return (value, slope)


def long_tables(lon_count, wave_count):
    lon_cells = jnp.arange(lon_count, dtype=jnp.int32)
    numbers = jnp.arange(wave_count, dtype=jnp.int32)
    angles = jnp.mod(numbers[:, None] * lon_cells[None, :], lon_count).astype(jnp.float32) * (
        2.0 * math.pi / lon_count
    )
    forward = jnp.stack([jnp.cos(angles), -jnp.sin(angles)]) / math.sqrt(lon_count)
    factor = jnp.where(numbers == 0, 1.0, 2.0).astype(jnp.float32)
    inverse = forward * factor[None, :, None]
    return (forward.astype(jnp.bfloat16), inverse.astype(jnp.bfloat16))


def latitude_tables(mode_count, latitudes, lat_count):
    mode_index = jnp.arange(mode_count, dtype=jnp.int32)
    signed = jnp.where(mode_index < mode_count // 2, mode_index, mode_index - mode_count)
    angles = jnp.mod(signed[:, None] * latitudes[None, :], lat_count).astype(jnp.float32) * (
        2.0 * math.pi / lat_count
    )
    scaled = 1.0 / math.sqrt(lat_count)
    return (
        (jnp.cos(angles) * scaled).astype(jnp.bfloat16),
        (jnp.sin(angles) * scaled).astype(jnp.bfloat16),
    )


def long_forward(field_in, long_table):
    return jnp.einsum("pkw,rwc->prkc", long_table, field_in, preferred_element_type=jnp.float32)


def long_inverse(spectrum, long_table):
    return jnp.einsum("pkw,prkc->rwc", long_table, spectrum, preferred_element_type=jnp.float32)


def lat_forward(cos_table, sin_table, real_part, imag_part):

    def multiply(table, operand):
        return jnp.einsum("qh,hkc->qkc", table, operand, preferred_element_type=jnp.float32)

    out_real = multiply(cos_table, real_part) + multiply(sin_table, imag_part)
    out_imag = multiply(cos_table, imag_part) - multiply(sin_table, real_part)
    return (out_real, out_imag)


def lat_inverse(cos_table, sin_table, real_part, imag_part):

    def multiply(table, operand):
        return jnp.einsum("qh,qkc->hkc", table, operand, preferred_element_type=jnp.float32)

    out_real = multiply(cos_table, real_part) - multiply(sin_table, imag_part)
    out_imag = multiply(sin_table, real_part) + multiply(cos_table, imag_part)
    return (out_real, out_imag)


def block_product(real_part, imag_part, layer_mats):
    block_count, block_size = (layer_mats.shape[1], layer_mats.shape[2])
    real_part = real_part.reshape(-1, block_count, block_size)
    imag_part = imag_part.reshape(-1, block_count, block_size)

    def multiply(operand, matrix):
        return jnp.einsum("mni,nio->mno", operand, matrix, preferred_element_type=jnp.float32)

    out_real = multiply(real_part, layer_mats[0]) - multiply(imag_part, layer_mats[1])
    out_imag = multiply(real_part, layer_mats[1]) + multiply(imag_part, layer_mats[0])
    return (
        out_real.reshape(-1, block_count * block_size),
        out_imag.reshape(-1, block_count * block_size),
    )


def block_adjoint(real_part, imag_part, layer_mats):
    block_count, block_size = (layer_mats.shape[1], layer_mats.shape[2])
    real_part = real_part.reshape(-1, block_count, block_size)
    imag_part = imag_part.reshape(-1, block_count, block_size)

    def multiply(operand, matrix):
        return jnp.einsum("mno,nio->mni", operand, matrix, preferred_element_type=jnp.float32)

    out_real = multiply(real_part, layer_mats[0]) + multiply(imag_part, layer_mats[1])
    out_imag = multiply(imag_part, layer_mats[0]) - multiply(real_part, layer_mats[1])
    return (
        out_real.reshape(-1, block_count * block_size),
        out_imag.reshape(-1, block_count * block_size),
    )


def block_weight_grad(in_real, in_imag, cot_real, cot_imag, block_count):
    block_size = in_real.shape[1] // block_count
    in_real = in_real.reshape(-1, block_count, block_size)
    in_imag = in_imag.reshape(-1, block_count, block_size)
    cot_real = cot_real.reshape(-1, block_count, block_size)
    cot_imag = cot_imag.reshape(-1, block_count, block_size)

    def multiply(operand, matrix):
        return jnp.einsum("mni,mno->nio", operand, matrix, preferred_element_type=jnp.float32)

    grad_real = multiply(in_real, cot_real) + multiply(in_imag, cot_imag)
    grad_imag = multiply(in_real, cot_imag) - multiply(in_imag, cot_real)
    return jnp.stack([grad_real, grad_imag])


def body(fields, cotangent, norm_gain, weights, biases, cutoffs):
    field_in = fields[0]
    grad_out = cotangent[0]
    row_count, lon_count, channels = field_in.shape
    block_count = weights.shape[2]
    row_devices = lax.axis_size("row")
    row_index = lax.axis_index("row")
    lat_count = row_count * row_devices
    mode_count = cutoffs.shape[0]
    col_count = KW // row_devices
    members = lax.axis_size("dp") * fields.shape[0]
    fwd_long, inv_long = long_tables(lon_count, KW)
    lat_cos, lat_sin = latitude_tables(
        mode_count, jnp.arange(lat_count, dtype=jnp.int32), lat_count
    )
    wave_ids = row_index * col_count + jnp.arange(col_count, dtype=jnp.int32)
    kept_mask = (wave_ids[None, :] < cutoffs[:, None]).astype(jnp.float32)[:, :, None]
    spec_shape = (mode_count, col_count, channels)
    kept_rows = kept_mask.reshape(-1, 1)

    def send_waves(local):
        return lax.all_to_all(local, "row", split_axis=2, concat_axis=1, tiled=True)

    def spectral_input(arrived):
        real_part, imag_part = lat_forward(lat_cos, lat_sin, arrived[0], arrived[1])
        real_part = (real_part * kept_mask).astype(jnp.bfloat16).reshape(-1, channels)
        imag_part = (imag_part * kept_mask).astype(jnp.bfloat16).reshape(-1, channels)
        return (real_part, imag_part)

    def from_spectrum(real_part, imag_part):
        back_real, back_imag = lat_inverse(
            lat_cos, lat_sin, real_part.reshape(spec_shape), imag_part.reshape(spec_shape)
        )
        back_stack = jnp.stack([back_real, back_imag]).astype(jnp.bfloat16)
        return lax.all_to_all(back_stack, "row", split_axis=1, concat_axis=2, tiled=True)

    center = field_in.astype(jnp.float32)
    average = jnp.mean(center, axis=-1, keepdims=True)
    deviation = center - average
    inverse_std = lax.rsqrt(jnp.mean(deviation * deviation, axis=-1, keepdims=True) + norm_eps)
    normal = deviation * inverse_std
    normed = (normal * norm_gain).astype(jnp.bfloat16)
    spectrum = long_forward(normed, fwd_long).astype(jnp.bfloat16)
    cospectrum = long_forward(grad_out, inv_long).astype(jnp.bfloat16)
    arrived_input = send_waves(spectrum)
    in_real, in_imag = spectral_input(arrived_input)
    lifted_real, lifted_imag = block_product(in_real, in_imag, weights[0])
    lifted_real = lifted_real + biases[0, 0]
    lifted_imag = lifted_imag + biases[0, 1]
    act_real, slope_real = gelu_pair(lifted_real)
    act_imag, slope_imag = gelu_pair(lifted_imag)
    hidden_real = act_real.astype(jnp.bfloat16)
    hidden_imag = act_imag.astype(jnp.bfloat16)
    output_real, output_imag = block_product(hidden_real, hidden_imag, weights[1])
    output_real = output_real + biases[1, 0]
    output_imag = output_imag + biases[1, 1]
    shrunk_real = (output_real * kept_rows).astype(jnp.bfloat16)
    shrunk_imag = (output_imag * kept_rows).astype(jnp.bfloat16)
    returned = from_spectrum(shrunk_real, shrunk_imag)
    block_out = (center + long_inverse(returned, inv_long)).astype(jnp.bfloat16)
    grad_arrived = send_waves(cospectrum)
    upper_real, upper_imag = spectral_input(grad_arrived)
    second_grad = block_weight_grad(hidden_real, hidden_imag, upper_real, upper_imag, block_count)
    second_bias = jnp.stack(
        [
            jnp.sum(upper_real.astype(jnp.float32), axis=0),
            jnp.sum(upper_imag.astype(jnp.float32), axis=0),
        ]
    )
    middle_real, middle_imag = block_adjoint(upper_real, upper_imag, weights[1])
    lower_real = (middle_real * slope_real).astype(jnp.bfloat16)
    lower_imag = (middle_imag * slope_imag).astype(jnp.bfloat16)
    first_grad = block_weight_grad(in_real, in_imag, lower_real, lower_imag, block_count)
    first_bias = jnp.stack(
        [
            jnp.sum(lower_real.astype(jnp.float32), axis=0),
            jnp.sum(lower_imag.astype(jnp.float32), axis=0),
        ]
    )
    bottom_real, bottom_imag = block_adjoint(lower_real, lower_imag, weights[0])
    bottom_real = (bottom_real * kept_rows).astype(jnp.bfloat16)
    bottom_imag = (bottom_imag * kept_rows).astype(jnp.bfloat16)
    bottom_stack = from_spectrum(bottom_real, bottom_imag)
    normed_grad = long_inverse(bottom_stack, fwd_long)
    gain_part = jnp.sum(normed_grad * normal, axis=(0, 1))
    scaled = normed_grad * norm_gain
    dfield = inverse_std * (
        scaled
        - jnp.mean(scaled, axis=-1, keepdims=True)
        - normal * jnp.mean(scaled * normal, axis=-1, keepdims=True)
    )
    input_grad = (grad_out.astype(jnp.float32) + dfield).astype(jnp.bfloat16)
    spectral_scale = 1.0 / math.sqrt(members * mode_count * KW)
    gain_scale = 1.0 / math.sqrt(members * lat_count * lon_count)
    local_sums = (
        jnp.stack([first_grad, second_grad]) * spectral_scale,
        jnp.stack([first_bias, second_bias]) * spectral_scale,
        gain_part * gain_scale,
    )
    totals = lax.psum((local_sums[0], local_sums[1], local_sums[2]), ("dp", "row"))
    return (block_out[None], input_grad[None], totals[0], totals[1], totals[2])


def solution(mesh):
    placed = (P("dp", "row", None, None), P("dp", "row", None, None), P(), P(), P(), P())
    return jax.shard_map(
        body,
        mesh=mesh,
        in_specs=placed,
        out_specs=(P("dp", "row", None, None), P("dp", "row", None, None), P(), P(), P()),
        check_vma=False,
    )
```

profile of v0, /device:TPU:6, one launch (start us, length us, event | category | flops | bytes accessed | tf_op | source)
XLA Modules:
  0.0 444.1 jit_solution(17467837603418170227)
XLA Ops:
  7.2 1.1 sine_negate_fusion
  8.3 3.3 convert_reduce_fusion
  11.6 1.6 fusion.15
  13.3 3.8 convert_bitcast_fusion.2
  17.1 5.4 %copy.139 = bf16[2,8,176,768]{3,0,1,2:T(2,128)(2,1)} copy(bf16[2,8,176,768]{3,2,0,1:T(8,128)(2,1)S(1)} %convert_bitcast_fusion.2) | data formatting | bytes 8650752 | tf_op jit(solution)/shard_map/convert_element_type | solution.py:167
  22.5 8.9 %all-to-all-start = ((bf16[2,8,176,768]{3,0,1,2:T(2,128)(2,1)}), bf16[2,8,176,768]{3,0,1,2:T(2,128)(2,1)}, u32[]{:S(2)}, u32[]{:S(2)}) async-start(bf16[2,8,176,768]{3,0,1,2:T(2,128)(2,1)} %copy.139), calls=%async_computation | async-start | bytes 8650752 | tf_op jit(solution)/shard_map/all_to_all | solution.py:146
  31.4 4.7 %convert_bitcast_fusion.1 = bf16[2,8,176,768]{3,2,1,0:T(8,128)(2,1)S(1)} fusion(bf16[1,8,360,768]{3,2,1,0:T(8,128)(2,1)} %param.7, f32[1,176,360]{2,1,0:T(8,128)S(1)} %get-tuple-element.31, f32[1,176,360]{2,1,0:T(8,128)S(1)} %get-tuple-element.32, f32[176]{0:T(256)S(1)} %fusion.235), kind=kOutput, calls=%fused_computation.40 | convolution fusion | flops 1559678208 | bytes 9256640 | tf_op jit(solution)/shard_map/pkw,rwc->prkc/dot_general | solution.py:51
  36.1 3.6 copy.157
  39.7 42.0 %all-to-all-done = bf16[2,8,176,768]{3,0,1,2:T(2,128)(2,1)} async-done(((bf16[2,8,176,768]{3,0,1,2:T(2,128)(2,1)}), bf16[2,8,176,768]{3,0,1,2:T(2,128)(2,1)}, u32[]{:S(2)}, u32[]{:S(2)}) %all-to-all-start) | async-done | bytes 4325408 | tf_op jit(solution)/shard_map/all_to_all | solution.py:146
  81.8 7.2 %all-to-all-start.2 = ((bf16[2,8,176,768]{3,1,0,2:T(8,128)(2,1)}), bf16[2,8,176,768]{3,1,0,2:T(8,128)(2,1)}, u32[]{:S(2)}, u32[]{:S(2)}) async-start(bf16[2,8,176,768]{3,1,0,2:T(8,128)(2,1)} %copy.157), calls=%async_computation.2 | async-start | bytes 8650752 | tf_op jit(solution)/shard_map/all_to_all | solution.py:146
  89.2 2.8 copy.140
  92.0 1.6 fusion.329
  94.7 44.9 %all-to-all-done.2 = bf16[2,8,176,768]{3,1,0,2:T(8,128)(2,1)} async-done(((bf16[2,8,176,768]{3,1,0,2:T(8,128)(2,1)}), bf16[2,8,176,768]{3,1,0,2:T(8,128)(2,1)}, u32[]{:S(2)}, u32[]{:S(2)}) %all-to-all-start.2) | async-done | bytes 4325408 | tf_op jit(solution)/shard_map/all_to_all | solution.py:146
  139.6 2.5 copy.158
  142.4 1.3 fusion.38
  143.7 1.3 fusion.40
  146.1 2.1 fusion.165
  148.2 2.1 fusion.167
  150.3 2.1 fusion.107
  153.0 1.7 convert_reduce_fusion.3
  155.5 1.4 reshape_reshape.19
  156.9 2.0 fusion.148
  159.0 1.6 convert_reduce_fusion.4
  161.1 1.3 fusion.155
  162.4 2.5 multiply_convert_fusion
  164.9 1.8 convert_reduce_fusion.1
  166.7 1.1 fusion.183
  167.8 1.2 multiply_convert_fusion.1
  170.8 2.9 fusion.226
  173.7 2.9 fusion.215
  177.7 3.3 fusion.64
  182.6 6.5 %copy.171 = bf16[2,128,11,768]{3,0,2,1:T(2,128)(2,1)} copy(bf16[2,128,11,768]{3,1,2,0:T(8,128)(2,1)S(1)} %pad_maximum_fusion.1) | data formatting | bytes 8650752 | tf_op jit(solution)/shard_map/stack | solution.py:158
  189.1 7.6 %all-to-all-start.3 = ((bf16[2,128,11,768]{3,0,2,1:T(2,128)(2,1)}), bf16[2,128,11,768]{3,0,2,1:T(2,128)(2,1)}, u32[]{:S(2)}, u32[]{:S(2)}) async-start(bf16[2,128,11,768]{3,0,2,1:T(2,128)(2,1)} %copy.171), calls=%async_computation.3 | async-start | bytes 8650752 | tf_op jit(solution)/shard_map/all_to_all | solution.py:159
  198.7 1.4 reshape.265
  205.5 6.5 %copy.153 = bf16[2,128,11,768]{3,0,2,1:T(2,128)(2,1)} copy(bf16[2,128,11,768]{3,1,2,0:T(8,128)(2,1)S(1)} %pad_maximum_fusion) | data formatting | bytes 8650752 | tf_op jit(solution)/shard_map/stack | solution.py:158
  212.0 35.2 %all-to-all-done.3 = bf16[2,128,11,768]{3,0,2,1:T(2,128)(2,1)} async-done(((bf16[2,128,11,768]{3,0,2,1:T(2,128)(2,1)}), bf16[2,128,11,768]{3,0,2,1:T(2,128)(2,1)}, u32[]{:S(2)}, u32[]{:S(2)}) %all-to-all-start.3) | async-done | bytes 4325408 | tf_op jit(solution)/shard_map/all_to_all | solution.py:159
  247.2 7.2 %all-to-all-start.1 = ((bf16[2,128,11,768]{3,0,2,1:T(2,128)(2,1)}), bf16[2,128,11,768]{3,0,2,1:T(2,128)(2,1)}, u32[]{:S(2)}, u32[]{:S(2)}) async-start(bf16[2,128,11,768]{3,0,2,1:T(2,128)(2,1)} %copy.153), calls=%async_computation.1 | async-start | bytes 8650752 | tf_op jit(solution)/shard_map/all_to_all | solution.py:159
  257.7 1.4 maximum_multiply_fusion
  259.2 3.2 copy.321
  263.5 7.0 %fusion.14 = (f32[768]{0:T(1024)S(1)}, f32[8,360]{1,0:T(8,128)S(1)}, f32[8,360]{1,0:T(8,128)S(1)}, f32[8,768,360,1]{1,2,3,0:T(8,128)}) fusion(bf16[1,8,360,768]{3,2,1,0:T(8,128)(2,1)S(1)} %bitcast.300, f32[8,360]{1,0:T(8,128)S(1)} %add_rsqrt_fusion, f32[8,360]{1,0:T(8,128)S(1)} %broadcast_multiply_fusion.2, f32[768]{0:T(1024)S(1)} %copy-done.25, ...), kind=kOutput, calls=%fused_computation.16 | convolution fusion | flops 1577415680 | bytes 18155520 | tf_op jit(solution)/shard_map/pkw,prkc->rwc/dot_general | solution.py:55
  270.5 36.3 %all-to-all-done.1 = bf16[2,128,11,768]{3,0,2,1:T(2,128)(2,1)} async-done(((bf16[2,128,11,768]{3,0,2,1:T(2,128)(2,1)}), bf16[2,128,11,768]{3,0,2,1:T(2,128)(2,1)}, u32[]{:S(2)}, u32[]{:S(2)}) %all-to-all-start.1) | async-done | bytes 4325408 | tf_op jit(solution)/shard_map/all_to_all | solution.py:159
  306.8 3.1 copy.322
  309.9 2.3 copy.155
  312.3 66.1 %all-reduce = (f32[2,2,768]{2,1,0:T(2,128)}, f32[768]{0:T(1024)}) all-reduce(f32[2,2,768]{2,1,0:T(2,128)S(1)} %maximum_multiply_fusion.1, f32[768]{0:T(1024)S(1)} %broadcast_multiply_fusion.3), channel_id=1, replica_groups=mesh['dp'=8,'row'=16] {'dp','row'}, use_global_device_ids=true, to_apply=%region_9.10 | all-reduce | flops 3840 | bytes 30720 | tf_op jit(solution)/shard_map/psum | solution.py:224
  378.4 11.1 %fusion.19 = bf16[1,8,360,768]{3,2,1,0:T(8,128)(2,1)} fusion(bf16[1,8,360,768]{3,2,1,0:T(8,128)(2,1)} %param.6, f32[8,768,360,1]{1,2,3,0:T(8,128)} %get-tuple-element.22, bf16[1,8,360,768]{3,2,1,0:T(8,128)(2,1)} %param.7, f32[8,360]{1,0:T(8,128)S(1)} %broadcast_multiply_fusion, f32[8,360]{1,0:T(8,128)S(1)} %broadcast_multiply_fusion.1, ...), kind=kLoop, calls=%fused_computation.22 | loop fusion | flops 24330240 | bytes 22167552 | tf_op jit(solution)/shard_map/broadcast_in_dim | solution.py:225
  389.5 5.1 %fusion.18 = bf16[1,8,360,768]{3,2,1,0:T(8,128)(2,1)} fusion(bf16[1,8,360,768]{3,2,1,0:T(8,128)(2,1)S(1)} %bitcast.302, bf16[2,8,176,768]{3,1,2,0:T(8,128)(2,1)S(1)} %bitcast.307, f32[1,176,360]{2,1,0:T(8,128)S(1)} %copy-done.20, f32[1,176,360]{2,1,0:T(8,128)S(1)} %copy-done.22, f32[176]{0:T(256)S(1)} %fusion.235), kind=kOutput, calls=%fused_computation.21 | convolution fusion | flops 1564151040 | bytes 13680320 | tf_op jit(solution)/shard_map/pkw,prkc->rwc/dot_general | solution.py:55
  394.5 39.6 %all-reduce.3.cloned.1.call-done = f32[2,2,8,96,96]{4,3,2,1,0:T(8,128)} async-done(((f32[2,2,8,96,96]{4,3,2,1,0:T(8,128)}), f32[2,2,8,96,96]{4,3,2,1,0:T(8,128)}) %all-reduce.3.cloned.1.call-update) | async-done | bytes 1179664 | tf_op jit(solution)/shard_map/psum | solution.py:224
  434.2 2.7 copy.324
  (129 shorter events, 20.5 us)
Async XLA Ops:
  7.2 4.5 %copy-start = (bf16[1,8,360,768]{3,2,1,0:T(8,128)(2,1)S(1)}, bf16[1,8,360,768]{3,2,1,0:T(8,128)(2,1)}, u32[]{:S(2)}) copy-start(bf16[1,8,360,768]{3,2,1,0:T(8,128)(2,1)} %param.6) | copy-start | bytes 13271044
  8.3 23.1 %copy-start.19 = (f32[1,176,360]{2,1,0:T(8,128)}, f32[1,176,360]{2,1,0:T(8,128)S(1)}, u32[]{:S(2)}) copy-start(f32[1,176,360]{2,1,0:T(8,128)S(1)} %get-tuple-element.31) | copy-start | bytes 760324
  8.3 23.1 %copy-start.21 = (f32[1,176,360]{2,1,0:T(8,128)}, f32[1,176,360]{2,1,0:T(8,128)S(1)}, u32[]{:S(2)}) copy-start(f32[1,176,360]{2,1,0:T(8,128)S(1)} %get-tuple-element.32) | copy-start | bytes 760324
  8.3 4.9 %copy-start.25 = (f32[768]{0:T(1024)S(1)}, f32[768]{0:T(1024)}, u32[]{:S(2)}) copy-start(f32[768]{0:T(1024)} %param.8) | copy-start | bytes 9220
  22.5 59.3 %all-to-all-start = ((bf16[2,8,176,768]{3,0,1,2:T(2,128)(2,1)}), bf16[2,8,176,768]{3,0,1,2:T(2,128)(2,1)}, u32[]{:S(2)}, u32[]{:S(2)}) async-start(bf16[2,8,176,768]{3,0,1,2:T(2,128)(2,1)} %copy.139), calls=%async_computation | async-start | bytes 8650752 | tf_op jit(solution)/shard_map/all_to_all | solution.py:146
  39.7 49.2 %copy-start.24 = (f32[2,2,768]{2,1,0:T(2,128)S(1)}, f32[2,2,768]{2,1,0:T(2,128)}, u32[]{:S(2)}) copy-start(f32[2,2,768]{2,1,0:T(2,128)} %param.10) | copy-start | bytes 36868
  39.7 49.4 %copy-start.26 = (s32[16]{0:T(128)S(1)}, s32[16]{0:T(128)}, u32[]{:S(2)}) copy-start(s32[16]{0:T(128)} %param.11) | copy-start | bytes 196
  81.8 57.8 %all-to-all-start.2 = ((bf16[2,8,176,768]{3,1,0,2:T(8,128)(2,1)}), bf16[2,8,176,768]{3,1,0,2:T(8,128)(2,1)}, u32[]{:S(2)}, u32[]{:S(2)}) async-start(bf16[2,8,176,768]{3,1,0,2:T(8,128)(2,1)} %copy.157), calls=%async_computation.2 | async-start | bytes 8650752 | tf_op jit(solution)/shard_map/all_to_all | solution.py:146
  142.4 2.6 copy-start.1
  152.9 14.8 %copy-start.16 = (bf16[176,8,96]{2,1,0:T(8,128)(2,1)}, bf16[176,8,96]{2,1,0:T(8,128)(2,1)S(1)}, u32[]{:S(2)}) copy-start(bf16[176,8,96]{2,1,0:T(8,128)(2,1)S(1)} %reshape_reshape.17) | copy-start | bytes 811012
  160.6 4.3 copy-start.3
  161.1 6.7 %copy-start.5 = (bf16[176,8,96]{2,1,0:T(8,128)(2,1)}, bf16[176,8,96]{2,1,0:T(8,128)(2,1)S(1)}, u32[]{:S(2)}) copy-start(bf16[176,8,96]{2,1,0:T(8,128)(2,1)S(1)} %reshape_reshape.18) | copy-start | bytes 811012
  162.4 5.4 %copy-start.23 = (f32[8,176,96]{2,1,0:T(8,128)S(1)}, f32[8,176,96]{2,1,0:T(8,128)}, u32[]{:S(2)}) copy-start(f32[8,176,96]{2,1,0:T(8,128)} %fusion.167) | copy-start | bytes 1622020
  166.7 3.2 copy-start.9
  169.6 7.0 %copy-start.11 = (bf16[176,8,96]{2,0,1:T(8,128)(2,1)}, bf16[176,8,96]{2,0,1:T(8,128)(2,1)S(1)}, u32[]{:S(2)}) copy-start(bf16[176,8,96]{2,0,1:T(8,128)(2,1)S(1)} %get-tuple-element.30) | copy-start | bytes 811012
  170.8 5.9 %copy-start.18 = (f32[8,176,96]{2,1,0:T(8,128)S(1)}, f32[8,176,96]{2,1,0:T(8,128)}, u32[]{:S(2)}) copy-start(f32[8,176,96]{2,1,0:T(8,128)} %fusion.183) | copy-start | bytes 1622020
  177.7 3.5 copy-start.2
  189.1 7.8 %copy-start.4 = (bf16[2,2,8,96,96]{4,3,2,1,0:T(8,128)(2,1)S(1)}, bf16[2,2,8,96,96]{4,3,2,1,0:T(8,128)(2,1)}, u32[]{:S(2)}) copy-start(bf16[2,2,8,96,96]{4,3,2,1,0:T(8,128)(2,1)} %param.9) | copy-start | bytes 1769476
  189.1 7.8 %copy-start.7 = (bf16[176,8,96]{2,0,1:T(8,128)(2,1)S(1)}, bf16[176,8,96]{2,0,1:T(8,128)(2,1)}, u32[]{:S(2)}) copy-start(bf16[176,8,96]{2,0,1:T(8,128)(2,1)} %get-tuple-element.18) | copy-start | bytes 811012
  189.1 8.2 %copy-start.13 = (bf16[176,8,96]{2,0,1:T(8,128)(2,1)S(1)}, bf16[176,8,96]{2,0,1:T(8,128)(2,1)}, u32[]{:S(2)}) copy-start(bf16[176,8,96]{2,0,1:T(8,128)(2,1)} %get-tuple-element.20) | copy-start | bytes 811012
  189.1 58.1 %all-to-all-start.3 = ((bf16[2,128,11,768]{3,0,2,1:T(2,128)(2,1)}), bf16[2,128,11,768]{3,0,2,1:T(2,128)(2,1)}, u32[]{:S(2)}, u32[]{:S(2)}) async-start(bf16[2,128,11,768]{3,0,2,1:T(2,128)(2,1)} %copy.171), calls=%async_computation.3 | async-start | bytes 8650752 | tf_op jit(solution)/shard_map/all_to_all | solution.py:159
  212.0 42.7 %copy-start.12 = (bf16[176,8,96]{2,0,1:T(8,128)(2,1)S(1)}, bf16[176,8,96]{2,0,1:T(8,128)(2,1)}, u32[]{:S(2)}) copy-start(bf16[176,8,96]{2,0,1:T(8,128)(2,1)} %copy-done.11) | copy-start | bytes 811012
  212.0 43.0 %copy-start.10 = (bf16[176,8,96]{2,0,1:T(8,128)(2,1)S(1)}, bf16[176,8,96]{2,0,1:T(8,128)(2,1)}, u32[]{:S(2)}) copy-start(bf16[176,8,96]{2,0,1:T(8,128)(2,1)} %copy-done.9) | copy-start | bytes 811012
  212.0 43.1 %copy-start.17 = (bf16[176,8,96]{2,1,0:T(8,128)(2,1)S(1)}, bf16[176,8,96]{2,1,0:T(8,128)(2,1)}, u32[]{:S(2)}) copy-start(bf16[176,8,96]{2,1,0:T(8,128)(2,1)} %copy-done.16) | copy-start | bytes 811012
  247.2 59.6 %all-to-all-start.1 = ((bf16[2,128,11,768]{3,0,2,1:T(2,128)(2,1)}), bf16[2,128,11,768]{3,0,2,1:T(2,128)(2,1)}, u32[]{:S(2)}, u32[]{:S(2)}) async-start(bf16[2,128,11,768]{3,0,2,1:T(2,128)(2,1)} %copy.153), calls=%async_computation.1 | async-start | bytes 8650752 | tf_op jit(solution)/shard_map/all_to_all | solution.py:159
  254.4 1.8 copy-start.8
  254.4 2.2 copy-start.6
  254.4 2.2 copy-start.14
  254.4 179.7 %all-reduce.3.cloned.1.call-start = ((), (), s32[]{:S(2)}) async-start(), calls=%async_computation.4 | async-start | bytes 3145728 | tf_op jit(solution)/shard_map/psum | solution.py:224
  259.1 3.5 slice-start
  262.3 1.0 slice-start.1
  262.3 1.1 copy-start.20
  262.3 1.2 copy-start.22
  309.9 79.5 %slice-start.2 = ((s8[4423680]{0:T(1024)(128)(4,1)}), s8[229376]{0:T(1024)(128)(4,1)S(1)}, s32[]{:S(2)}) async-start(s8[4423680]{0:T(1024)(128)(4,1)} %bitcast.301), calls=%async_computation.7 | async-start | bytes 458752
  378.4 11.1 %slice-start.3 = ((s8[4423680]{0:T(1024)(128)(4,1)}), s8[4194304]{0:T(1024)(128)(4,1)S(1)}, s32[]{:S(2)}) async-start(s8[4423680]{0:T(1024)(128)(4,1)} %bitcast.301), calls=%async_computation.8 | async-start | bytes 8388608
  378.4 11.1 %copy-start.15 = (bf16[2,8,16,11,768]{4,1,3,2,0:T(8,128)(2,1)S(1)}, bf16[2,8,16,11,768]{4,1,3,2,0:T(8,128)(2,1)}, u32[]{:S(2)}) copy-start(bf16[2,8,16,11,768]{4,1,3,2,0:T(8,128)(2,1)} %copy.155) | copy-start | bytes 12976132
Sparse Core Ops, SparseCore 0:
  260.5 173.5 all-reduce.2
where the time goes:
time: 453 us; the launch traced here: 444 us
  waiting for transfers between devices  198 us (44%)
  blocking collectives  66.1 us (15%)
  matrix products  63.7 us (14%)
  local copies, waits for them, and re-layouts  50.2 us (11%)
  starting transfers between devices  31.2 us (7%)
  other arithmetic  19.5 us (4%)
  between operations  15.2 us (3%)
    all_to_all x2, waiting for transfers between devices, send_waves(): return lax.all_to_all(local, 'row', split_axis=2, concat_axis=1, tiled=True)  87 us
    all_to_all x2, waiting for transfers between devices, from_spectrum(): lax.all_to_all(back_stack, 'row', split_axis=1, concat_axis=2, tiled=True)  71.5 us
    psum x1, blocking collectives, body(): lax.psum((local_sums[0], local_sums[1], local_sums[2]), ('dp', 'row'))  66.1 us
    psum x1, waiting for transfers between devices, body(): lax.psum((local_sums[0], local_sums[1], local_sums[2]), ('dp', 'row'))  39.6 us
    all_to_all x2, starting transfers between devices, send_waves(): return lax.all_to_all(local, 'row', split_axis=2, concat_axis=1, tiled=True)  16.1 us
    all_to_all x2, starting transfers between devices, from_spectrum(): lax.all_to_all(back_stack, 'row', split_axis=1, concat_axis=2, tiled=True)  14.8 us
    dot_general x8, matrix products, multiply(): jnp.einsum('qh,qkc->hkc', table, operand, preferred_element_type=jnp.floa...  13.8 us
    another operation x2, local copies, waits for them, and re-layouts, from_spectrum(): back_stack = jnp.stack([back_real, back_imag]).astype(jnp.bfloat16)  13 us
  transfers between devices with their start and end apart: 5, of which 5 were waited for; matrix products, arithmetic and copies ran while one was open for 15% of the time, Pallas kernels for 0%

commit v1 on v0

v1 whole, which is shorter than its diff:
```python
import functools
import math

import jax
import jax.numpy as jnp
import ml_dtypes
import numpy as np
from jax import lax
from jax.experimental import pallas as pl
from jax.experimental.pallas import tpu as pltpu
from jax.sharding import PartitionSpec as P

C = 768
NB = 8
BS = 96
W = 360
KW = 176
H = 128
KH = 16
ENS = 8

ROWS = 8
WB = 8
COLS = KW // WB // 2
UNITS = COLS * KH
GC = C // 2
GB = NB // 2
AXES = ("dp", "row")

norm_eps = 1e-06
gelu_coef = 0.7978845608
cube_coef = 0.044715
bf16 = jnp.bfloat16
f32 = jnp.float32
VMEM_LIMIT = 48 * 1024 * 1024


def long_tables():
    ids = np.arange(KW).reshape(COLS, 2, WB).transpose(1, 0, 2)
    angle = ((ids[..., None] * np.arange(W)) % W).astype(np.float64) * (2.0 * math.pi / W)
    forward = np.stack([np.cos(angle), -np.sin(angle)], axis=2).astype(np.float32)
    forward = forward / np.float32(math.sqrt(W))
    factor = np.where(ids == 0, 1.0, 2.0).astype(np.float32)[:, :, None, :, None]
    forward, inverse = (
        table.reshape(2, COLS * 2 * WB, W).astype(ml_dtypes.bfloat16)
        for table in (forward, forward * factor)
    )
    return forward, inverse


def latitude_table():
    modes = np.arange(KH)
    signed = np.where(modes < KH // 2, modes, modes - KH)
    angle = ((signed[:, None] * np.arange(H)) % H).astype(np.float64) * (2.0 * math.pi / H)
    cos = (np.cos(angle) / math.sqrt(H)).astype(np.float32).reshape(KH, H // ROWS, ROWS)
    sin = (np.sin(angle) / math.sqrt(H)).astype(np.float32).reshape(KH, H // ROWS, ROWS)
    mixed = np.stack([np.stack([cos, sin], -1), np.stack([-sin, cos], -1)], 1)
    whole = np.einsum("jprhq,kl->rjpkhql", mixed, np.eye(WB, dtype=np.float32))
    return whole.reshape(H // ROWS, KH * 2 * WB, ROWS * 2 * WB).astype(ml_dtypes.bfloat16)


def place(index):
    dp, row = divmod(index, 16)
    y, x_lo = divmod(dp, 2)
    z, rest = divmod(row, 4)
    x_hi, core = divmod(rest, 2)
    return x_hi * 2 + x_lo, y, z, core


def number(x, y, z, core):
    return (y * 2 + x % 2) * 16 + z * 4 + (x // 2) * 2 + core


def shift(array, dx=0, dz=0):
    pairs = []
    for index in range(128):
        x, y, z, core = place(index)
        pairs.append((index, number((x + dx) % 4, y, (z + dz) % 4, core)))
    return lax.ppermute(array, AXES, pairs)


def swap(array, fx=0, fy=0, fz=0, fc=0):
    pairs = []
    for index in range(128):
        x, y, z, core = place(index)
        pairs.append((index, number(x ^ fx, y ^ fy, z ^ fz, core ^ fc)))
    return lax.ppermute(array, AXES, pairs)


def call(kernel, name, grid, in_specs, out_specs, out_shape, scratch=(), flops=0, moved=0):
    return pl.pallas_call(
        kernel,
        name=name,
        grid_spec=pltpu.PrefetchScalarGridSpec(
            num_scalar_prefetch=3,
            grid=grid,
            in_specs=in_specs,
            out_specs=out_specs,
            scratch_shapes=list(scratch),
        ),
        out_shape=out_shape,
        compiler_params=pltpu.CompilerParams(vmem_limit_bytes=VMEM_LIMIT),
        cost_estimate=pl.CostEstimate(flops=flops, bytes_accessed=moved, transcendentals=0),
    )


def layer_norm(block):
    center = block.astype(f32)
    deviation = center - jnp.mean(center, axis=-1, keepdims=True)
    inverse_std = lax.rsqrt(jnp.mean(deviation * deviation, axis=-1, keepdims=True) + norm_eps)
    return deviation * inverse_std, inverse_std


def dot(left, right):
    return jnp.dot(left, right, preferred_element_type=f32)


def dot_nt(left, right):
    return lax.dot_general(left, right, (((1,), (1,)), ((), ())), preferred_element_type=f32)


def dot_tn(left, right):
    return lax.dot_general(left, right, (((0,), (0,)), ((), ())), preferred_element_type=f32)


def own_table(shape):
    return pl.BlockSpec((1,) + shape, lambda i, info, slots, cuts: (info[2], 0, 0))


def beside_table(shape):
    return pl.BlockSpec((1,) + shape, lambda i, info, slots, cuts: (1 - info[2], 0, 0))


def row_block(*shape):
    zeros = (0,) * len(shape)
    return pl.BlockSpec((1,) + shape, lambda i, info, slots, cuts: (i,) + zeros)


def fixed(*shape):
    zeros = (0,) * len(shape)
    return pl.BlockSpec(shape, lambda i, info, slots, cuts: zeros)


def lon_forward(scalars, array, table, gain=None):
    def kernel(info, slots, cuts, own_t, beside_t, x, *rest):
        if gain is None:
            own, beside = rest
            rows = x[0]
        else:
            scale, own, beside = rest
            rows = (layer_norm(x[0])[0] * scale[...]).astype(bf16)
        own[0] = dot(own_t[0], rows).astype(bf16).reshape(COLS, 2 * WB, C)
        beside[0] = dot(beside_t[0], rows).astype(bf16).reshape(COLS, 2 * WB, C)

    specs = [own_table((KW, W)), beside_table((KW, W)), row_block(W, C)]
    operands = [table, table, array]
    if gain is not None:
        specs.append(fixed(1, C))
        operands.append(gain)
    shape = jax.ShapeDtypeStruct((ROWS, COLS, 2 * WB, C), bf16)
    return call(
        kernel,
        "lon_forward",
        (ROWS,),
        specs,
        [row_block(COLS, 2 * WB, C)] * 2,
        [shape, shape],
        flops=2 * ROWS * 2 * KW * W * C,
        moved=2 * ROWS * C * (W + 2 * KW),
    )(*scalars, *operands)


def lane_block(lanes, *shape):
    zeros = (0,) * len(shape)
    return pl.BlockSpec(shape + (lanes,), lambda i, info, slots, cuts: zeros + (i,))


def lat_tables(shape):
    return [
        pl.BlockSpec((1,) + shape, lambda i, info, slots, cuts: (info[3], 0, 0)),
        pl.BlockSpec((1,) + shape, lambda i, info, slots, cuts: (info[4], 0, 0)),
    ]


LANES = 256


def slot_base(info, step, half, owned):
    return (lax.rem(info[0] + step, 4) * 2 + lax.rem(info[1] + half, 2)) * owned


def lat_forward(scalars, own, beside, table, owned):
    def kernel(info, slots, cuts, own_t, beside_t, x_own, x_beside, *rest):
        outs, units = rest[:8], rest[8]
        mix = jnp.concatenate([own_t[0], beside_t[0]], axis=1)
        for col in range(COLS):
            rows = jnp.concatenate(
                [x_own[:, col].reshape(-1, LANES), x_beside[:, col].reshape(-1, LANES)], axis=0
            )
            units[col * KH : (col + 1) * KH] = dot(mix, rows).astype(bf16).reshape(KH, 2 * WB, LANES)
        units[UNITS] = jnp.zeros((2 * WB, LANES), bf16)
        for step in range(4):
            for half in range(2):
                base = slot_base(info, step, half, owned)
                for at in range(owned):
                    outs[step * 2 + half][at] = units[slots[base + at]]

    shape = jax.ShapeDtypeStruct((owned, 2 * WB, C), bf16)
    return call(
        kernel,
        "lat_forward",
        (C // LANES,),
        lat_tables((KH * 2 * WB, ROWS * 2 * WB)) + [lane_block(LANES, ROWS, COLS, 2 * WB)] * 2,
        [lane_block(LANES, owned, 2 * WB)] * 8,
        [shape] * 8,
        [pltpu.VMEM((UNITS + 1, 2 * WB, LANES), bf16)],
        flops=2 * 256 * 256 * C * COLS,
        moved=2 * C * 16 * (UNITS + 8 * owned),
    )(*scalars, table, table, own, beside)


def lat_inverse(scalars, pieces, table, owned):
    def kernel(info, slots, cuts, own_t, beside_t, *rest):
        arrived, (own, beside, units) = rest[:8], rest[8:]
        units[...] = jnp.zeros(units.shape, bf16)
        for step in range(4):
            for half in range(2):
                base = slot_base(info, step, half, owned)
                for at in range(owned):
                    units[slots[base + at]] = arrived[step * 2 + half][at]
        mix = jnp.concatenate([own_t[0], beside_t[0]], axis=0)
        for col in range(COLS):
            rows = dot(mix, units[col * KH : (col + 1) * KH].reshape(-1, LANES)).astype(bf16)
            half = ROWS * 2 * WB
            own[:, col] = rows[:half].reshape(ROWS, 2 * WB, LANES)
            beside[:, col] = rows[half:].reshape(ROWS, 2 * WB, LANES)

    shape = jax.ShapeDtypeStruct((ROWS, COLS, 2 * WB, C), bf16)
    return call(
        kernel,
        "lat_inverse",
        (C // LANES,),
        lat_tables((ROWS * 2 * WB, KH * 2 * WB)) + [lane_block(LANES, owned, 2 * WB)] * 8,
        [lane_block(LANES, ROWS, COLS, 2 * WB)] * 2,
        [shape, shape],
        [pltpu.VMEM((UNITS + 1, 2 * WB, LANES), bf16)],
        flops=2 * 256 * 256 * C * COLS,
        moved=2 * C * 16 * (UNITS + 8 * owned),
    )(*scalars, table, table, *pieces)


def lon_inverse_fields(scalars, own, beside, table, fields):
    def kernel(info, slots, cuts, own_t, beside_t, x_own, x_beside, x, out):
        grid = dot(own_t[0], x_own[0].reshape(KW, C)) + dot(beside_t[0], x_beside[0].reshape(KW, C))
        out[0] = (x[0].astype(f32) + grid).astype(bf16)

    return call(
        kernel,
        "lon_inverse_fields",
        (ROWS,),
        [own_table((W, KW)), beside_table((W, KW))]
        + [row_block(COLS, 2 * WB, C)] * 2
        + [row_block(W, C)],
        row_block(W, C),
        jax.ShapeDtypeStruct((ROWS, W, C), bf16),
        flops=2 * ROWS * 2 * KW * W * C,
        moved=2 * ROWS * C * (2 * W + 2 * KW),
    )(*scalars, table, table, own, beside, fields)


def lon_inverse_grad(scalars, own, beside, table, fields, cotangent, gain):
    def kernel(info, slots, cuts, own_t, beside_t, x_own, x_beside, x, cot, scale, out):
        grid = dot(own_t[0], x_own[0].reshape(KW, C)) + dot(beside_t[0], x_beside[0].reshape(KW, C))
        normal, inverse_std = layer_norm(x[0])
        scaled = grid * scale[...]
        first = jnp.mean(scaled, axis=-1, keepdims=True)
        second = jnp.mean(scaled * normal, axis=-1, keepdims=True)
        grad = inverse_std * (scaled - first - normal * second)
        out[0] = (cot[0].astype(f32) + grad).astype(bf16)

    return call(
        kernel,
        "lon_inverse_grad",
        (ROWS,),
        [own_table((W, KW)), beside_table((W, KW))]
        + [row_block(COLS, 2 * WB, C)] * 2
        + [row_block(W, C)] * 2
        + [fixed(1, C)],
        row_block(W, C),
        jax.ShapeDtypeStruct((ROWS, W, C), bf16),
        flops=2 * ROWS * 2 * KW * W * C,
        moved=2 * ROWS * C * (3 * W + 2 * KW),
    )(*scalars, table, table, own, beside, fields, cotangent, gain)


def wide_weights(scalars, weights):
    def kernel(info, slots, cuts, w, out):
        row = lax.broadcasted_iota(jnp.int32, (BS, GC), 0)
        lane = lax.broadcasted_iota(jnp.int32, (BS, GC), 1)
        for layer in range(2):
            for block in range(GB):
                move = (lane == row + block * BS).astype(f32).astype(bf16)
                real = dot(w[layer, 0, block], move)
                imag = dot(w[layer, 1, block], move)
                top = slice(block * BS, (block + 1) * BS)
                low = slice(GC + block * BS, GC + (block + 1) * BS)
                out[layer, 0, top, :GC] = real.astype(bf16)
                out[layer, 0, top, GC:] = imag.astype(bf16)
                out[layer, 0, low, :GC] = (-imag).astype(bf16)
                out[layer, 0, low, GC:] = real.astype(bf16)

    return call(
        kernel,
        "wide_weights",
        (2,),
        [pl.BlockSpec((2, 2, GB, BS, BS), lambda i, info, slots, cuts: (0, 0, i, 0, 0))],
        pl.BlockSpec((2, 1, C, C), lambda i, info, slots, cuts: (0, i, 0, 0)),
        jax.ShapeDtypeStruct((2, 2, C, C), bf16),
        moved=2 * 5 * C * C,
    )(*scalars, weights)


def gelu_pair(values):
    inner = jnp.tanh(gelu_coef * (values + cube_coef * values * values * values))
    value = 0.5 * values * (1.0 + inner)
    slope = 0.5 * (1.0 + inner) + 0.5 * values * (1.0 - inner * inner) * gelu_coef * (
        1.0 + 3.0 * cube_coef * values * values
    )
    return (value, slope)


def kept_of(info, slots, cuts, at, owned):
    unit = slots[(info[0] * 2 + info[5]) * owned + at]
    first = WB * (2 * lax.div(unit, KH) + info[2])
    return jnp.where(unit < UNITS, cuts[lax.rem(unit, KH)] - first, 0)


def gather_units(info, slots, cuts, left, right, held, owned):
    row = lax.broadcasted_iota(jnp.int32, (WB, GC), 0)
    for at in range(owned):
        unit = left[at].astype(f32) + right[at].astype(f32)
        kept = row < kept_of(info, slots, cuts, at, owned)
        rows = slice(at * WB, (at + 1) * WB)
        held[rows, :GC] = jnp.where(kept, unit[:WB], 0.0)
        held[rows, GC:] = jnp.where(kept, unit[WB:], 0.0)
    return held[...].astype(bf16)


def scatter_units(info, slots, cuts, held, out, owned):
    row = lax.broadcasted_iota(jnp.int32, (WB, GC), 0)
    for at in range(owned):
        kept = row < kept_of(info, slots, cuts, at, owned)
        rows = slice(at * WB, (at + 1) * WB)
        real = jnp.where(kept, held[rows, :GC], 0.0)
        imag = jnp.where(kept, held[rows, GC:], 0.0)
        out[at] = jnp.concatenate([real, imag], axis=0).astype(bf16)


def group_block(rows):
    return pl.BlockSpec((1, rows, C), lambda i, info, slots, cuts: (i, 0, 0))


def weight_block(layer):
    return pl.BlockSpec((1, 1, C, C), lambda i, info, slots, cuts: (layer, i, 0, 0))


def spectral_forward(scalars, left, right, wide, biases, owned):
    count = owned * WB

    def kernel(info, slots, cuts, xl, xr, w0, w1, bias, out, given, hidden, slope, held):
        given[0] = gather_units(info, slots, cuts, xl, xr, held, owned)
        b0 = jnp.concatenate([bias[0, 0:1, :], bias[0, 1:2, :]], axis=1)
        b1 = jnp.concatenate([bias[1, 0:1, :], bias[1, 1:2, :]], axis=1)
        act, slope[0] = gelu_pair(dot(given[0], w0[0, 0]) + b0)
        hidden[0] = act.astype(bf16)
        held[...] = dot(hidden[0], w1[0, 0]) + b1
        scatter_units(info, slots, cuts, held, out, owned)

    return call(
        kernel,
        "spectral_forward",
        (2,),
        [lane_block(GC, owned, 2 * WB)] * 2
        + [weight_block(0), weight_block(1), lane_block(GC, 2, 2)],
        [lane_block(GC, owned, 2 * WB)] + [group_block(count)] * 3,
        [jax.ShapeDtypeStruct((owned, 2 * WB, C), bf16)]
        + [jax.ShapeDtypeStruct((2, count, C), kind) for kind in (bf16, bf16, f32)],
        [pltpu.VMEM((count, C), f32)],
        flops=8 * count * C * C,
        moved=8 * C * C + 20 * count * C,
    )(*scalars, left, right, wide, wide, biases)


def spectral_backward(scalars, left, right, wide, given, slope, owned):
    count = owned * WB

    def kernel(info, slots, cuts, xl, xr, w0, w1, given, slope, out, upper, lower, sums, held):
        upper[0] = gather_units(info, slots, cuts, xl, xr, held, owned)
        sums[0] = jnp.zeros(sums.shape[1:], f32)
        sums[0, 0:1, :] = jnp.sum(upper[0].astype(f32), axis=0, keepdims=True)
        low = (dot_nt(upper[0], w1[0, 0]) * slope[0]).astype(bf16)
        lower[0] = low
        sums[0, 1:2, :] = jnp.sum(low.astype(f32), axis=0, keepdims=True)
        held[...] = dot_nt(low, w0[0, 0])
        scatter_units(info, slots, cuts, held, out, owned)
        sums[0, 2:3, :] = jnp.sum(held[...] * given[0].astype(f32), axis=0, keepdims=True)

    return call(
        kernel,
        "spectral_backward",
        (2,),
        [lane_block(GC, owned, 2 * WB)] * 2
        + [weight_block(0), weight_block(1), group_block(count), group_block(count)],
        [lane_block(GC, owned, 2 * WB)] + [group_block(count)] * 2 + [group_block(8)],
        [jax.ShapeDtypeStruct((owned, 2 * WB, C), bf16)]
        + [jax.ShapeDtypeStruct((2, count, C), bf16)] * 2
        + [jax.ShapeDtypeStruct((2, 8, C), f32)],
        [pltpu.VMEM((count, C), f32)],
        flops=8 * count * C * C,
        moved=8 * C * C + 20 * count * C,
    )(*scalars, left, right, wide, wide, given, slope)


SHARE = 416


def weight_sums(scalars, given, lower, hidden, upper, sums, owned):
    count = owned * WB

    def kernel(info, slots, cuts, u0, y0, u1, y1, small, out):
        lane = lax.div(lax.broadcasted_iota(jnp.int32, (BS, GC), 1), BS)
        for layer, (u, y) in enumerate(((u0, y0), (u1, y1))):
            whole = dot_tn(u[0], y[0])
            real = whole[:GC, :GC] + whole[GC:, GC:]
            imag = whole[:GC, GC:] - whole[GC:, :GC]
            for part, value in enumerate((real, imag)):
                folded = value[:BS]
                for block in range(1, GB):
                    folded = jnp.where(lane == block, value[block * BS : (block + 1) * BS], folded)
                first = (layer * 2 + part) * BS
                out[0, first : first + BS, :] = folded
        out[0, 4 * BS : 4 * BS + 8, :] = small[0, :, :GC]
        out[0, 4 * BS + 8 : 4 * BS + 16, :] = small[0, :, GC:]
        out[0, 4 * BS + 16 :, :] = jnp.zeros((SHARE - 4 * BS - 16, GC), f32)

    return call(
        kernel,
        "weight_sums",
        (2,),
        [group_block(count)] * 4 + [group_block(8)],
        pl.BlockSpec((1, SHARE, GC), lambda i, info, slots, cuts: (i, 0, 0)),
        jax.ShapeDtypeStruct((2, SHARE, GC), f32),
        flops=8 * count * C * C,
        moved=8 * count * C * 2 + 8 * SHARE * GC,
    )(*scalars, given, lower, hidden, upper, sums)


def halves(array, bit):
    size = array.shape[0] // 2
    keep = lax.dynamic_slice_in_dim(array, bit * size, size, 0)
    send = lax.dynamic_slice_in_dim(array, (1 - bit) * size, size, 0)
    return keep, send


def joined(array, other, bit):
    first = jnp.where(bit == 0, array, other)
    second = jnp.where(bit == 0, other, array)
    return jnp.concatenate([first, second], axis=0)


def sum_everywhere(array, core, y):
    steps = [(core, dict(fc=1)), (lax.div(y, 2), dict(fy=2)), (lax.rem(y, 2), dict(fy=1))]
    for bit, flip in steps:
        keep, send = halves(array, bit)
        array = keep + swap(send, **flip)
    for flip in (dict(fz=1), dict(fz=2), dict(fx=1), dict(fx=2)):
        array = array + swap(array, **flip)
    for bit, flip in reversed(steps):
        array = joined(array, swap(array, **flip), bit)
    return array


def add(*arrays):
    total = arrays[0].astype(f32)
    for array in arrays[1:]:
        total = total + array.astype(f32)
    return total.astype(bf16)


def to_owners(parts):
    own_a, own_b, up_a, up_b, far_a, far_b, down_a, down_b = parts
    from_down = shift(far_a, dz=1)
    from_up = shift(far_b, dz=-1)
    near_b = shift(up_b, dz=1)
    near_a = shift(down_a, dz=-1)
    last_a = shift(add(up_a, from_down), dz=1)
    last_b = shift(add(down_b, from_up), dz=-1)
    left = shift(add(own_a, near_a, last_a), dx=1)
    right = shift(add(own_b, near_b, last_b), dx=-1)
    return left, right


def to_rows(result):
    own_a = shift(result, dx=-1)
    own_b = shift(result, dx=1)
    down_a = shift(own_a, dz=1)
    up_b = shift(own_b, dz=-1)
    down_b = shift(own_b, dz=1)
    up_a = shift(own_a, dz=-1)
    far_a = shift(down_a, dz=1)
    far_b = shift(up_b, dz=-1)
    return own_a, own_b, up_a, up_b, far_a, far_b, down_a, down_b


def unit_slots(cutoffs, core, total):
    unit = jnp.arange(UNITS, dtype=jnp.int32)
    first = WB * (2 * (unit // KH) + core)
    kept = (jnp.tile(cutoffs, COLS) > first).astype(jnp.int32)
    rank = jnp.sum(jnp.where(unit[None, :] <= unit[:, None], kept[None, :], 0), axis=1)
    place_of = jnp.arange(total, dtype=jnp.int32)
    return jnp.sum((rank[None, :] <= place_of[:, None]).astype(jnp.int32), axis=1)


def body(fields, cotangent, norm_gain, weights, biases, cutoffs):
    field_in = fields[0]
    grad_out = cotangent[0]
    dp = lax.axis_index("dp").astype(jnp.int32)
    row = lax.axis_index("row").astype(jnp.int32)
    z, x_hi, core = row // 4, (row // 2) % 2, row % 2
    y, x_lo = dp // 2, dp % 2
    x = x_hi * 2 + x_lo
    half_owned = ((x + 3) % 4) // 2
    beside_row = row + 1 - 2 * core
    zero = jnp.zeros((), jnp.int32)
    info = jnp.stack([z, x_hi, core, row, beside_row, half_owned, zero, zero])
    owned = UNITS // 8
    slots = unit_slots(cutoffs, core, 8 * owned)
    scalars = (info, slots, cutoffs)
    fwd_table, inv_table = long_tables()
    fwd_turned = jnp.asarray(fwd_table.transpose(0, 2, 1))
    inv_turned = jnp.asarray(inv_table.transpose(0, 2, 1))
    fwd_table, inv_table = jnp.asarray(fwd_table), jnp.asarray(inv_table)
    lat_np = latitude_table()
    lat_table = jnp.asarray(lat_np)
    lat_turned = jnp.asarray(lat_np.transpose(0, 2, 1))
    gain = norm_gain.reshape(1, C)

    f_own, f_send = lon_forward(scalars, field_in, fwd_table, gain)
    f_recv = swap(f_send, fc=1)
    g_own, g_send = lon_forward(scalars, grad_out, inv_table)
    g_recv = swap(g_send, fc=1)
    f_parts = lat_forward(scalars, f_own, f_recv, lat_table, owned)
    f_left, f_right = to_owners(f_parts)
    g_parts = lat_forward(scalars, g_own, g_recv, lat_table, owned)
    wide = wide_weights(scalars, weights)
    shrunk, given, hidden, slope = spectral_forward(scalars, f_left, f_right, wide, biases, owned)
    g_left, g_right = to_owners(g_parts)
    f_pieces = to_rows(shrunk)
    bottom, upper, lower, sums = spectral_backward(
        scalars, g_left, g_right, wide, given, slope, owned
    )
    g_pieces = to_rows(bottom)
    shares = weight_sums(scalars, given, lower, hidden, upper, sums, owned)
    totals = sum_everywhere(shares.reshape(2 * SHARE, GC), core, y).reshape(2, SHARE, GC)
    f_own, f_send = lat_inverse(scalars, f_pieces, lat_turned, owned)
    f_recv = swap(f_send, fc=1)
    block_out = lon_inverse_fields(scalars, f_own, f_recv, inv_turned, field_in)
    g_own, g_send = lat_inverse(scalars, g_pieces, lat_turned, owned)
    g_recv = swap(g_send, fc=1)
    input_grad = lon_inverse_grad(
        scalars, g_own, g_recv, fwd_turned, field_in, grad_out, gain
    )

    spectral_scale = 1.0 / math.sqrt(ENS * KH * KW)
    gain_scale = 1.0 / math.sqrt(ENS * H * W)
    weight_grads = totals[:, : 4 * BS].reshape(2, 2, 2, BS, GB, BS) * spectral_scale
    weight_grads = weight_grads.transpose(1, 2, 0, 4, 3, 5).reshape(2, 2, NB, BS, BS)
    small = totals[:, 4 * BS : 4 * BS + 16].reshape(2, 2, 8, GC).transpose(2, 1, 0, 3).reshape(8, 2, C)
    bias_grads = jnp.stack([small[1], small[0]]) * spectral_scale
    gain_grad = (small[2, 0] + small[2, 1]) * gain_scale / norm_gain
    return (block_out[None], input_grad[None], weight_grads, bias_grads, gain_grad)


def solution(mesh):
    placed = (P("dp", "row", None, None), P("dp", "row", None, None), P(), P(), P(), P())
    return jax.shard_map(
        body,
        mesh=mesh,
        in_specs=placed,
        out_specs=(P("dp", "row", None, None), P("dp", "row", None, None), P(), P(), P()),
        check_vma=False,
    )
```

time: 453 us -> 296 us (0.65); the launches traced: 444 us -> 293 us
  waiting for transfers between devices: 198 us -> 118 us
  Pallas kernels: 0 us -> 73.4 us
  blocking collectives: 66.1 us -> 0 us
  matrix products: 63.7 us -> 0 us
  starting transfers between devices: 31.2 us -> 67.9 us
  local copies, waits for them, and re-layouts: 50.2 us -> 20.7 us
  between operations: 15.2 us -> 1.17 us
  other arithmetic: 19.5 us -> 11.9 us
    all_to_all x4 -> x0, waiting for transfers between devices: 159 us -> none  [the longest x2 87 us: send_waves(): return lax.all_to_all(local, 'row', split_axis=2, concat_axis=1, tiled=True)]
    ppermute x0 -> x46, waiting for transfers between devices: none -> 118 us  [the longest x32 95.6 us: shift(): return lax.ppermute(array, AXES, pairs)]
    pallas_call x0 -> x12, Pallas kernels: none -> 73.4 us  [the longest x2 15.8 us: lon_forward(): call(kernel, 'lon_forward', (ROWS,), specs, [row_block(COLS, 2 * WB, C)]...]
    ppermute x0 -> x46, starting transfers between devices: none -> 67.9 us  [the longest x32 46.9 us: shift(): return lax.ppermute(array, AXES, pairs)]
    psum x1 -> x0, blocking collectives: 66.1 us -> none  [body(): lax.psum((local_sums[0], local_sums[1], local_sums[2]), ('dp', 'row'))]
    dot_general x44 -> x0, matrix products: 63.7 us -> none  [the longest x8 13.8 us: multiply(): jnp.einsum('qh,qkc->hkc', table, operand, preferred_element_type=jnp.floa...]
    psum x1 -> x0, waiting for transfers between devices: 39.6 us -> none  [body(): lax.psum((local_sums[0], local_sums[1], local_sums[2]), ('dp', 'row'))]
    all_to_all x4 -> x0, starting transfers between devices: 30.9 us -> none  [the longest x2 16.1 us: send_waves(): return lax.all_to_all(local, 'row', split_axis=2, concat_axis=1, tiled=True)]
  transfers between devices with their start and end apart: 5 -> 46, of which waited for: 5 -> 24; matrix products, arithmetic and copies ran while one was open for 15% -> 6% of each run, Pallas kernels for 0% -> 17%
where the time goes in v1:
time: 296 us; the launch traced here: 293 us
  waiting for transfers between devices  118 us (40%)
  Pallas kernels  73.4 us (25%)
  starting transfers between devices  67.9 us (23%)
  local copies, waits for them, and re-layouts  20.7 us (7%)
  other arithmetic  11.9 us (4%)
    ppermute x32, waiting for transfers between devices, shift(): return lax.ppermute(array, AXES, pairs)  95.6 us
    ppermute x32, starting transfers between devices, shift(): return lax.ppermute(array, AXES, pairs)  46.9 us
    ppermute x14, waiting for transfers between devices, swap(): return lax.ppermute(array, AXES, pairs)  22.2 us
    ppermute x14, starting transfers between devices, swap(): return lax.ppermute(array, AXES, pairs)  21 us
    pallas_call x2, Pallas kernels, lon_forward(): call(kernel, 'lon_forward', (ROWS,), specs, [row_block(COLS, 2 * WB, C)]...  15.8 us
    unnamed x55, local copies, waits for them, and re-layouts  13.6 us
    pallas_call x2, Pallas kernels, lat_inverse(): call(kernel, 'lat_inverse', (C // LANES,), lat_tables((ROWS * 2 * WB, KH...  13.3 us
    pallas_call x1, Pallas kernels, lon_inverse_grad(): call(kernel, 'lon_inverse_grad', (ROWS,), [own_table((W, KW)), beside_tab...  11.3 us
  transfers between devices with their start and end apart: 46, of which 24 were waited for; matrix products, arithmetic and copies ran while one was open for 6% of the time, Pallas kernels for 17%

profile of v1, /device:TPU:6, one launch (start us, length us, event | category | flops | bytes accessed | tf_op | source)
XLA Modules:
  0.0 292.7 jit_solution(1670049255240503525)
XLA Ops:
  3.4 7.2 %lon_forward.3 = (bf16[8,11,16,768]{3,2,1,0:T(8,128)(2,1)S(1)}, bf16[8,11,16,768]{3,2,1,0:T(8,128)(2,1)S(1)}) custom-call(s32[8]{0:T(128)S(1)} %stack.30.info, s32[176]{0:T(256)S(1)} %convert_reduce_fusion.slots, s32[16]{0:T(128)S(1)} %copy-done.12, bf16[2,176,360]{2,1,0:T(8,128)(2,1)S(1)} %copy-done.16, bf16[2,176,360]{2,1,0:T(8,128)(2,1)S(1)} %copy-done.16, ...), custom_call_target="tpu_custom_call" | custom-call | flops 1557135360 | bytes 8749056 | tf_op jit(solution)/shard_map/lon_forward/pallas_call | solution.py:161
  12.0 8.6 %lon_forward.2 = (bf16[8,11,16,768]{3,2,1,0:T(8,128)(2,1)S(1)}, bf16[8,11,16,768]{3,2,1,0:T(8,128)(2,1)S(1)}) custom-call(s32[8]{0:T(128)S(1)} %stack.30.info, s32[176]{0:T(256)S(1)} %convert_reduce_fusion.slots, s32[16]{0:T(128)S(1)} %copy-done.12, bf16[2,176,360]{2,1,0:T(8,128)(2,1)S(1)} %copy-done.15, bf16[2,176,360]{2,1,0:T(8,128)(2,1)S(1)} %copy-done.15, ...), custom_call_target="tpu_custom_call" | custom-call | flops 1557135360 | bytes 8749056 | tf_op jit(solution)/shard_map/lon_forward/pallas_call | solution.py:161
  23.8 5.0 %lat_forward.3 = (bf16[22,16,768]{2,1,0:T(8,128)(2,1)S(1)}, bf16[22,16,768]{2,1,0:T(8,128)(2,1)S(1)}, bf16[22,16,768]{2,1,0:T(8,128)(2,1)S(1)}, bf16[22,16,768]{...) custom-call(s32[8]{0:T(128)S(1)} %stack.30.info, ...), custom_call_target="tpu_custom_call" | custom-call | flops 1107296256 | bytes 8650752 | tf_op jit(solution)/shard_map/lat_forward/pallas_call | solution.py:209
  28.8 4.1 %collective-permute-start.24 = (bf16[22,16,768]{2,1,0:T(8,128)(2,1)S(1)}, bf16[22,16,768]{2,1,0:T(8,128)(2,1)S(1)}, u32[]{:S(2)}, u32[]{:S(2)}) collective-permute-start(bf16[22,16,768]{2,1,0:T(8,128)(2,1)S(1)} %get-tuple-element.59), channel_id=1, source_target_pairs={{0,12},{1,13},{2,14},{3,15},{4,0},{5,1},{6,2},{7,3},{8,4},{9,5},{1... | collective-permute-start | bytes 1622024 | tf_op jit(solution)/shard_map/ppermute | solution.py:79
  34.2 5.0 %lat_forward.2 = (bf16[22,16,768]{2,1,0:T(8,128)(2,1)S(1)}, bf16[22,16,768]{2,1,0:T(8,128)(2,1)S(1)}, bf16[22,16,768]{2,1,0:T(8,128)(2,1)S(1)}, bf16[22,16,768]{...) custom-call(s32[8]{0:T(128)S(1)} %stack.30.info, ...), custom_call_target="tpu_custom_call" | custom-call | flops 1107296256 | bytes 8650752 | tf_op jit(solution)/shard_map/lat_forward/pallas_call | solution.py:209
  39.2 3.3 %collective-permute-start.6 = (bf16[22,16,768]{2,1,0:T(8,128)(2,1)S(1)}, bf16[22,16,768]{2,1,0:T(8,128)(2,1)S(1)}, u32[]{:S(2)}, u32[]{:S(2)}) collective-permute-start(bf16[22,16,768]{2,1,0:T(8,128)(2,1)S(1)} %get-tuple-element.46), channel_id=1, source_target_pairs={{0,12},{1,13},{2,14},{3,15},{4,0},{5,1},{6,2},{7,3},{8,4},{9,5},{1... | collective-permute-start | bytes 1622024 | tf_op jit(solution)/shard_map/ppermute | solution.py:79
  42.5 3.2 %collective-permute-start.19 = (bf16[22,16,768]{2,1,0:T(8,128)(2,1)S(1)}, bf16[22,16,768]{2,1,0:T(8,128)(2,1)S(1)}, u32[]{:S(2)}, u32[]{:S(2)}) collective-permute-start(bf16[22,16,768]{2,1,0:T(8,128)(2,1)S(1)} %get-tuple-element.53), channel_id=1, source_target_pairs={{0,12},{1,13},{2,14},{3,15},{4,0},{5,1},{6,2},{7,3},{8,4},{9,5},{1... | collective-permute-start | bytes 1622024 | tf_op jit(solution)/shard_map/ppermute | solution.py:79
  46.0 3.3 %collective-permute-done.20 = bf16[22,16,768]{2,1,0:T(8,128)(2,1)S(1)} collective-permute-done((bf16[22,16,768]{2,1,0:T(8,128)(2,1)S(1)}, bf16[22,16,768]{2,1,0:T(8,128)(2,1)S(1)}, u32[]{:S(2)}, u32[]{:S(2)}) %collective-permute-start.20) | collective-permute-done | bytes 540704 | tf_op jit(solution)/shard_map/ppermute | solution.py:79
  49.6 7.5 %collective-permute-done.6 = bf16[22,16,768]{2,1,0:T(8,128)(2,1)S(1)} collective-permute-done((bf16[22,16,768]{2,1,0:T(8,128)(2,1)S(1)}, bf16[22,16,768]{2,1,0:T(8,128)(2,1)S(1)}, u32[]{:S(2)}, u32[]{:S(2)}) %collective-permute-start.6) | collective-permute-done | bytes 540704 | tf_op jit(solution)/shard_map/ppermute | solution.py:79
  57.6 14.8 %collective-permute-done.2 = bf16[22,16,768]{2,1,0:T(8,128)(2,1)S(1)} collective-permute-done((bf16[22,16,768]{2,1,0:T(8,128)(2,1)S(1)}, bf16[22,16,768]{2,1,0:T(8,128)(2,1)S(1)}, u32[]{:S(2)}, u32[]{:S(2)}) %collective-permute-start.2) | collective-permute-done | bytes 540704 | tf_op jit(solution)/shard_map/ppermute | solution.py:79
  72.7 7.6 %collective-permute-done.25 = bf16[22,16,768]{2,1,0:T(8,128)(2,1)S(1)} collective-permute-done((bf16[22,16,768]{2,1,0:T(8,128)(2,1)S(1)}, bf16[22,16,768]{2,1,0:T(8,128)(2,1)S(1)}, u32[]{:S(2)}, u32[]{:S(2)}) %collective-permute-start.25) | collective-permute-done | bytes 540704 | tf_op jit(solution)/shard_map/ppermute | solution.py:79
  82.9 9.0 %collective-permute-done.7 = bf16[22,16,768]{2,1,0:T(8,128)(2,1)S(1)} collective-permute-done((bf16[22,16,768]{2,1,0:T(8,128)(2,1)S(1)}, bf16[22,16,768]{2,1,0:T(8,128)(2,1)S(1)}, u32[]{:S(2)}, u32[]{:S(2)}) %collective-permute-start.7) | collective-permute-done | bytes 540704 | tf_op jit(solution)/shard_map/ppermute | solution.py:79
  93.7 8.8 %collective-permute-done.1 = bf16[22,16,768]{2,1,0:T(8,128)(2,1)S(1)} collective-permute-done((bf16[22,16,768]{2,1,0:T(8,128)(2,1)S(1)}, bf16[22,16,768]{2,1,0:T(8,128)(2,1)S(1)}, u32[]{:S(2)}, u32[]{:S(2)}) %collective-permute-start.1) | collective-permute-done | bytes 540704 | tf_op jit(solution)/shard_map/ppermute | solution.py:79
  104.4 2.4 collective-permute-start.4
  109.7 2.2 copy-done
  111.8 5.4 %collective-permute-done.8.xr = bf16[22,16,768]{2,1,0:T(8,128)(2,1)S(1)} collective-permute-done((bf16[22,16,768]{2,1,0:T(8,128)(2,1)}, bf16[22,16,768]{2,1,0:T(8,128)(2,1)S(1)}, u32[]{:S(2)}, u32[]{:S(2)}) %collective-permute-start.8) | collective-permute-done | bytes 540704 | tf_op jit(solution)/shard_map/ppermute | solution.py:79
  117.3 2.5 collective-permute-done.4.xl
  119.8 5.0 %spectral_forward.1 = (bf16[22,16,768]{2,1,0:T(8,128)(2,1)}, bf16[2,176,768]{2,1,0:T(8,128)(2,1)S(1)}, bf16[2,176,768]{2,1,0:T(8,128)(2,1)S(1)}, f32[2,176,768]{2,1,0:T(8,128)S(1)}) custom-call(s32[8]{0:T(128)S(1)} %stack.30.info, s32[176]{0:T(256)S(1)} %convert_reduce_fusion.slots, s32[16]{0:T(128)S(1)} %copy-done.13, ...), custom_call_target="tpu_custom_call" | custom-call | flops 830472192 | bytes 7421952 | tf_op jit(solution)/shard_map/spectral_forward/pallas_call | solution.py:379
  124.8 4.4 %collective-permute-done.22.xl = bf16[22,16,768]{2,1,0:T(8,128)(2,1)S(1)} collective-permute-done((bf16[22,16,768]{2,1,0:T(8,128)(2,1)}, bf16[22,16,768]{2,1,0:T(8,128)(2,1)S(1)}, u32[]{:S(2)}, u32[]{:S(2)}) %collective-permute-start.22) | collective-permute-done | bytes 540704 | tf_op jit(solution)/shard_map/ppermute | solution.py:79
  129.2 5.0 %spectral_backward.1 = (bf16[22,16,768]{2,1,0:T(8,128)(2,1)}, bf16[2,176,768]{2,1,0:T(8,128)(2,1)S(1)}, bf16[2,176,768]{2,1,0:T(8,128)(2,1)S(1)}, f32[2,8,768]{2,1,0:T(8,128)S(1)}) custom-call(s32[8]{0:T(128)S(1)} %stack.30.info, s32[176]{0:T(256)S(1)} %convert_reduce_fusion.slots, s32[16]{0:T(128)S(1)} %copy-done.13, ...), custom_call_target="tpu_custom_call" | custom-call | flops 830472192 | bytes 7421952 | tf_op jit(solution)/shard_map/spectral_backward/pallas_call | solution.py:408
  134.2 2.2 weight_sums.1
  138.7 3.3 %collective-permute-start.37 = (f32[208,384]{1,0:T(8,128)S(1)}, f32[208,384]{1,0:T(8,128)S(1)}, u32[]{:S(2)}, u32[]{:S(2)}) collective-permute-start(f32[208,384]{1,0:T(8,128)S(1)} %constant_dynamic-slice_fusion), channel_id=1, source_target_pairs={{0,64},{1,65},{2,66},{3,67},{4,68},{5,69},{6,70},{7,71},{8,72},{9,... | collective-permute-start | bytes 958472 | tf_op jit(solution)/shard_map/ppermute | solution.py:87
  142.0 7.9 %collective-permute-done.37 = f32[208,384]{1,0:T(8,128)S(1)} collective-permute-done((f32[208,384]{1,0:T(8,128)S(1)}, f32[208,384]{1,0:T(8,128)S(1)}, u32[]{:S(2)}, u32[]{:S(2)}) %collective-permute-start.37) | collective-permute-done | bytes 319520 | tf_op jit(solution)/shard_map/ppermute | solution.py:87
  151.6 3.7 %collective-permute-done.38 = f32[104,384]{1,0:T(8,128)S(1)} collective-permute-done((f32[104,384]{1,0:T(8,128)S(1)}, f32[104,384]{1,0:T(8,128)S(1)}, u32[]{:S(2)}, u32[]{:S(2)}) %collective-permute-start.38) | collective-permute-done | bytes 159776 | tf_op jit(solution)/shard_map/ppermute | solution.py:87
  156.7 3.1 %collective-permute-start.28 = (bf16[22,16,768]{2,1,0:T(8,128)(2,1)}, bf16[22,16,768]{2,1,0:T(8,128)(2,1)S(1)}, u32[]{:S(2)}, u32[]{:S(2)}) collective-permute-start(bf16[22,16,768]{2,1,0:T(8,128)(2,1)} %get-tuple-element.62), channel_id=1, source_target_pairs={{0,16},{1,17},{2,18},{3,19},{4,20},{5,21},{6,22},{7,23},{8,24},{9,... | collective-permute-start | bytes 1622024 | tf_op jit(solution)/shard_map/ppermute | solution.py:79
  160.8 4.0 %collective-permute-start.40 = (f32[104,384]{1,0:T(8,128)S(1)}, f32[104,384]{1,0:T(8,128)S(1)}, u32[]{:S(2)}, u32[]{:S(2)}) collective-permute-start(f32[104,384]{1,0:T(8,128)S(1)} %add.150), channel_id=1, source_target_pairs={{0,8},{1,9},{2,10},{3,11},{4,12},{5,13},{6,14},{7,15},{8,0},{9,1},... | collective-permute-start | bytes 479240 | tf_op jit(solution)/shard_map/ppermute | solution.py:87
  164.7 3.3 %collective-permute-done.40 = f32[104,384]{1,0:T(8,128)S(1)} collective-permute-done((f32[104,384]{1,0:T(8,128)S(1)}, f32[104,384]{1,0:T(8,128)S(1)}, u32[]{:S(2)}, u32[]{:S(2)}) %collective-permute-start.40) | collective-permute-done | bytes 159776 | tf_op jit(solution)/shard_map/ppermute | solution.py:87
  169.0 4.3 %collective-permute-done.41 = f32[104,384]{1,0:T(8,128)S(1)} collective-permute-done((f32[104,384]{1,0:T(8,128)S(1)}, f32[104,384]{1,0:T(8,128)S(1)}, u32[]{:S(2)}, u32[]{:S(2)}) %collective-permute-start.41) | collective-permute-done | bytes 159776 | tf_op jit(solution)/shard_map/ppermute | solution.py:87
  173.4 4.4 %collective-permute-start.42 = (f32[104,384]{1,0:T(8,128)S(1)}, f32[104,384]{1,0:T(8,128)S(1)}, u32[]{:S(2)}, u32[]{:S(2)}) collective-permute-start(f32[104,384]{1,0:T(8,128)S(1)} %add.152), channel_id=1, source_target_pairs={{0,2},{1,3},{2,0},{3,1},{4,6},{5,7},{6,4},{7,5},{8,10},{9,11},{10,... | collective-permute-start | bytes 479240 | tf_op jit(solution)/shard_map/ppermute | solution.py:87
  181.0 2.4 collective-permute-start.31
  183.4 3.1 %collective-permute-start.30 = (bf16[22,16,768]{2,1,0:T(8,128)(2,1)S(1)}, bf16[22,16,768]{2,1,0:T(8,128)(2,1)S(1)}, u32[]{:S(2)}, u32[]{:S(2)}) collective-permute-start(bf16[22,16,768]{2,1,0:T(8,128)(2,1)S(1)} %collective-permute-done.28.rest_1_), channel_id=1, source_target_pairs={{0,12},{1,13},{2,14},{3,15},{4,0},{5,1},{6,2},{7,3},{8,4},{9,5},{1... | collective-permute-start | bytes 1622024 | tf_op jit(solution)/shard_map/ppermute | solution.py:79
  188.5 3.6 %collective-permute-done.9.rest_0_ = bf16[22,16,768]{2,1,0:T(8,128)(2,1)} collective-permute-done((bf16[22,16,768]{2,1,0:T(8,128)(2,1)}, bf16[22,16,768]{2,1,0:T(8,128)(2,1)}, u32[]{:S(2)}, u32[]{:S(2)}) %collective-permute-start.9) | collective-permute-done | bytes 540704 | tf_op jit(solution)/shard_map/ppermute | solution.py:79
  193.8 3.0 %collective-permute-start.13 = (bf16[22,16,768]{2,1,0:T(8,128)(2,1)}, bf16[22,16,768]{2,1,0:T(8,128)(2,1)}, u32[]{:S(2)}, u32[]{:S(2)}) collective-permute-start(bf16[22,16,768]{2,1,0:T(8,128)(2,1)} %collective-permute-done.9.rest_0_), channel_id=1, source_target_pairs={{0,4},{1,5},{2,6},{3,7},{4,8},{5,9},{6,10},{7,11},{8,12},{9,13},{1... | collective-permute-start | bytes 1622024 | tf_op jit(solution)/shard_map/ppermute | solution.py:79
  196.7 2.5 collective-permute-done.30.rest_3_
  199.2 3.7 %collective-permute-start.12 = (bf16[22,16,768]{2,1,0:T(8,128)(2,1)}, bf16[22,16,768]{2,1,0:T(8,128)(2,1)}, u32[]{:S(2)}, u32[]{:S(2)}) collective-permute-start(bf16[22,16,768]{2,1,0:T(8,128)(2,1)} %collective-permute-done.10.rest_1_), channel_id=1, source_target_pairs={{0,12},{1,13},{2,14},{3,15},{4,0},{5,1},{6,2},{7,3},{8,4},{9,5},{1... | collective-permute-start | bytes 1622024 | tf_op jit(solution)/shard_map/ppermute | solution.py:79
  202.9 7.9 %collective-permute-done.29.rest_2_ = bf16[22,16,768]{2,1,0:T(8,128)(2,1)S(1)} collective-permute-done((bf16[22,16,768]{2,1,0:T(8,128)(2,1)S(1)}, bf16[22,16,768]{2,1,0:T(8,128)(2,1)S(1)}, u32[]{:S(2)}, u32[]{:S(2)}) %collective-permute-start.29) | collective-permute-done | bytes 540704 | tf_op jit(solution)/shard_map/ppermute | solution.py:79
  216.2 3.2 %collective-permute-start.44 = (f32[208,384]{1,0:T(8,128)}, f32[208,384]{1,0:T(8,128)S(1)}, u32[]{:S(2)}, u32[]{:S(2)}) collective-permute-start(f32[208,384]{1,0:T(8,128)} %pad_maximum_fusion.2), channel_id=1, source_target_pairs={{0,64},{1,65},{2,66},{3,67},{4,68},{5,69},{6,70},{7,71},{8,72},{9,... | collective-permute-start | bytes 958472 | tf_op jit(solution)/shard_map/ppermute | solution.py:87
  219.4 2.4 collective-permute-done.13.rest_6_
  224.3 9.0 %collective-permute-done.32.rest_4_ = bf16[22,16,768]{2,1,0:T(8,128)(2,1)} collective-permute-done((bf16[22,16,768]{2,1,0:T(8,128)(2,1)S(1)}, bf16[22,16,768]{2,1,0:T(8,128)(2,1)}, u32[]{:S(2)}, u32[]{:S(2)}) %collective-permute-start.32) | collective-permute-done | bytes 540704 | tf_op jit(solution)/shard_map/ppermute | solution.py:79
  234.0 3.8 %collective-permute-start.15 = (bf16[22,16,768]{2,1,0:T(8,128)(2,1)}, bf16[22,16,768]{2,1,0:T(8,128)(2,1)}, u32[]{:S(2)}, u32[]{:S(2)}) collective-permute-start(bf16[22,16,768]{2,1,0:T(8,128)(2,1)} %collective-permute-done.12.rest_3_), channel_id=1, source_target_pairs={{0,12},{1,13},{2,14},{3,15},{4,0},{5,1},{6,2},{7,3},{8,4},{9,5},{1... | collective-permute-start | bytes 1622024 | tf_op jit(solution)/shard_map/ppermute | solution.py:79
  238.8 6.1 %lat_inverse.3 = (bf16[8,11,16,768]{3,2,1,0:T(8,128)(2,1)}, bf16[8,11,16,768]{3,2,1,0:T(8,128)(2,1)}) custom-call(s32[8]{0:T(128)S(1)} %stack.30.info, s32[176]{0:T(256)S(1)} %convert_reduce_fusion.slots, s32[16]{0:T(128)S(1)} %copy-done.13, bf16[16,128,256]{2,1,0:T(8,128)(2,1)S(1)} %copy-done.1, bf16[16,128,256]{2,1,0:T(8,128)(2,1)S(1)} %copy-done.1, ...), custom_call_target="tpu_custom_call" | custom-call | flops 1107296256 | bytes 8650752 | tf_op jit(solution)/shard_map/lat_inverse/pallas_call | solution.py:239
  248.9 4.0 %collective-permute-done.14.rest_4_ = bf16[22,16,768]{2,1,0:T(8,128)(2,1)} collective-permute-done((bf16[22,16,768]{2,1,0:T(8,128)(2,1)}, bf16[22,16,768]{2,1,0:T(8,128)(2,1)}, u32[]{:S(2)}, u32[]{:S(2)}) %collective-permute-start.14) | collective-permute-done | bytes 540704 | tf_op jit(solution)/shard_map/ppermute | solution.py:79
  252.9 7.2 %lat_inverse.2 = (bf16[8,11,16,768]{3,2,1,0:T(8,128)(2,1)}, bf16[8,11,16,768]{3,2,1,0:T(8,128)(2,1)}) custom-call(s32[8]{0:T(128)S(1)} %stack.30.info, s32[176]{0:T(256)S(1)} %convert_reduce_fusion.slots, s32[16]{0:T(128)S(1)} %copy-done.13, bf16[16,128,256]{2,1,0:T(8,128)(2,1)S(1)} %copy-done.1, bf16[16,128,256]{2,1,0:T(8,128)(2,1)S(1)} %copy-done.1, ...), custom_call_target="tpu_custom_call" | custom-call | flops 1107296256 | bytes 8650752 | tf_op jit(solution)/shard_map/lat_inverse/pallas_call | solution.py:239
  262.6 2.4 slice_multiply_fusion
  264.9 3.2 %mul.82 = f32[2,2,2,96,4,96]{5,4,3,2,1,0:T(4,128)} reshape(f32[2,384,384]{2,1,0:T(8,128)} %slice_multiply_fusion) | data formatting | bytes 2359296 | tf_op jit(solution)/shard_map/mul | solution.py:576
  268.1 2.9 copy.21
  272.3 11.3 %lon_inverse_grad.1 = bf16[8,360,768]{2,1,0:T(8,128)(2,1)} custom-call(s32[8]{0:T(128)S(1)} %stack.30.info, s32[176]{0:T(256)S(1)} %convert_reduce_fusion.slots, s32[16]{0:T(128)S(1)} %copy-done.13, bf16[2,360,176]{2,1,0:T(8,128)(2,1)S(1)} %copy-done.8, bf16[2,360,176]{2,1,0:T(8,128)(2,1)S(1)} %copy-done.8, bf16[8,11,16,768]{3,2,1,0:T(8,128)(2,1)S(1)} %copy-done.3, ...), custom_call_target="tpu_custom_call" | custom-call | flops 1557135360 | bytes 17596416 | tf_op jit(solution)/shard_map/lon_inverse_grad/pallas_call | solution.py:281
  283.6 9.1 %lon_inverse_fields.1 = bf16[8,360,768]{2,1,0:T(8,128)(2,1)} custom-call(s32[8]{0:T(128)S(1)} %stack.30.info, s32[176]{0:T(256)S(1)} %convert_reduce_fusion.slots, s32[16]{0:T(128)S(1)} %copy-done.13, bf16[2,360,176]{2,1,0:T(8,128)(2,1)S(1)} %copy-done.7, bf16[2,360,176]{2,1,0:T(8,128)(2,1)S(1)} %copy-done.7, bf16[8,11,16,768]{3,2,1,0:T(8,128)(2,1)S(1)} %copy-done.6, ...), custom_call_target="tpu_custom_call" | custom-call | flops 1557135360 | bytes 13172736 | tf_op jit(solution)/shard_map/lon_inverse_fields/pallas_call | solution.py:257
  (155 shorter events, 50.3 us)
Async XLA Ops:
  12.0 10.5 %collective-permute-start.18 = (bf16[8,11,16,768]{3,2,1,0:T(8,128)(2,1)S(1)}, bf16[8,11,16,768]{3,2,1,0:T(8,128)(2,1)S(1)}, u32[]{:S(2)}, u32[]{:S(2)}) collective-permute-start(bf16[8,11,16,768]{3,2,1,0:T(8,128)(2,1)S(1)} %get-tuple-element.51), channel_id=1, source_target_pairs={{0,1},{1,0},{2,3},{3,2},{4,5},{5,4},{6,7},{7,6},{8,9},{9,8},{10,11... | collective-permute-start | bytes 6488072 | tf_op jit(solution)/shard_map/ppermute | solution.py:87
  21.9 10.9 %collective-permute-start = (bf16[8,11,16,768]{3,2,1,0:T(8,128)(2,1)S(1)}, bf16[8,11,16,768]{3,2,1,0:T(8,128)(2,1)S(1)}, u32[]{:S(2)}, u32[]{:S(2)}) collective-permute-start(bf16[8,11,16,768]{3,2,1,0:T(8,128)(2,1)S(1)} %get-tuple-element.38), channel_id=1, source_target_pairs={{0,1},{1,0},{2,3},{3,2},{4,5},{5,4},{6,7},{7,6},{8,9},{9,8},{10,11... | collective-permute-start | bytes 6488072 | tf_op jit(solution)/shard_map/ppermute | solution.py:87
  28.8 17.0 %collective-permute-start.24 = (bf16[22,16,768]{2,1,0:T(8,128)(2,1)S(1)}, bf16[22,16,768]{2,1,0:T(8,128)(2,1)S(1)}, u32[]{:S(2)}, u32[]{:S(2)}) collective-permute-start(bf16[22,16,768]{2,1,0:T(8,128)(2,1)S(1)} %get-tuple-element.59), channel_id=1, source_target_pairs={{0,12},{1,13},{2,14},{3,15},{4,0},{5,1},{6,2},{7,3},{8,4},{9,5},{1... | collective-permute-start | bytes 1622024 | tf_op jit(solution)/shard_map/ppermute | solution.py:79
  32.9 16.4 %collective-permute-start.20 = (bf16[22,16,768]{2,1,0:T(8,128)(2,1)S(1)}, bf16[22,16,768]{2,1,0:T(8,128)(2,1)S(1)}, u32[]{:S(2)}, u32[]{:S(2)}) collective-permute-start(bf16[22,16,768]{2,1,0:T(8,128)(2,1)S(1)} %get-tuple-element.55), channel_id=1, source_target_pairs={{0,4},{1,5},{2,6},{3,7},{4,8},{5,9},{6,10},{7,11},{8,12},{9,13},{1... | collective-permute-start | bytes 1622024 | tf_op jit(solution)/shard_map/ppermute | solution.py:79
  39.2 17.9 %collective-permute-start.6 = (bf16[22,16,768]{2,1,0:T(8,128)(2,1)S(1)}, bf16[22,16,768]{2,1,0:T(8,128)(2,1)S(1)}, u32[]{:S(2)}, u32[]{:S(2)}) collective-permute-start(bf16[22,16,768]{2,1,0:T(8,128)(2,1)S(1)} %get-tuple-element.46), channel_id=1, source_target_pairs={{0,12},{1,13},{2,14},{3,15},{4,0},{5,1},{6,2},{7,3},{8,4},{9,5},{1... | collective-permute-start | bytes 1622024 | tf_op jit(solution)/shard_map/ppermute | solution.py:79
  42.5 30.1 %collective-permute-start.23 = (bf16[22,16,768]{2,1,0:T(8,128)(2,1)S(1)}, bf16[22,16,768]{2,1,0:T(8,128)(2,1)S(1)}, u32[]{:S(2)}, u32[]{:S(2)}) collective-permute-start(bf16[22,16,768]{2,1,0:T(8,128)(2,1)S(1)} %get-tuple-element.57), channel_id=1, source_target_pairs={{0,4},{1,5},{2,6},{3,7},{4,8},{5,9},{6,10},{7,11},{8,12},{9,13},{1... | collective-permute-start | bytes 1622024 | tf_op jit(solution)/shard_map/ppermute | solution.py:79
  42.5 64.2 %collective-permute-start.19 = (bf16[22,16,768]{2,1,0:T(8,128)(2,1)S(1)}, bf16[22,16,768]{2,1,0:T(8,128)(2,1)S(1)}, u32[]{:S(2)}, u32[]{:S(2)}) collective-permute-start(bf16[22,16,768]{2,1,0:T(8,128)(2,1)S(1)} %get-tuple-element.53), channel_id=1, source_target_pairs={{0,12},{1,13},{2,14},{3,15},{4,0},{5,1},{6,2},{7,3},{8,4},{9,5},{1... | collective-permute-start | bytes 1622024 | tf_op jit(solution)/shard_map/ppermute | solution.py:79
  45.7 26.7 %collective-permute-start.2 = (bf16[22,16,768]{2,1,0:T(8,128)(2,1)S(1)}, bf16[22,16,768]{2,1,0:T(8,128)(2,1)S(1)}, u32[]{:S(2)}, u32[]{:S(2)}) collective-permute-start(bf16[22,16,768]{2,1,0:T(8,128)(2,1)S(1)} %get-tuple-element.42), channel_id=1, source_target_pairs={{0,4},{1,5},{2,6},{3,7},{4,8},{5,9},{6,10},{7,11},{8,12},{9,13},{1... | collective-permute-start | bytes 1622024 | tf_op jit(solution)/shard_map/ppermute | solution.py:79
  49.3 31.0 %collective-permute-start.25 = (bf16[22,16,768]{2,1,0:T(8,128)(2,1)S(1)}, bf16[22,16,768]{2,1,0:T(8,128)(2,1)S(1)}, u32[]{:S(2)}, u32[]{:S(2)}) collective-permute-start(bf16[22,16,768]{2,1,0:T(8,128)(2,1)S(1)} %add_convert_fusion.1), channel_id=1, source_target_pairs={{0,12},{1,13},{2,14},{3,15},{4,0},{5,1},{6,2},{7,3},{8,4},{9,5},{1... | collective-permute-start | bytes 1622024 | tf_op jit(solution)/shard_map/ppermute | solution.py:79
  57.1 25.6 %collective-permute-start.5 = (bf16[22,16,768]{2,1,0:T(8,128)(2,1)S(1)}, bf16[22,16,768]{2,1,0:T(8,128)(2,1)S(1)}, u32[]{:S(2)}, u32[]{:S(2)}) collective-permute-start(bf16[22,16,768]{2,1,0:T(8,128)(2,1)S(1)} %get-tuple-element.44), channel_id=1, source_target_pairs={{0,4},{1,5},{2,6},{3,7},{4,8},{5,9},{6,10},{7,11},{8,12},{9,13},{1... | collective-permute-start | bytes 1622024 | tf_op jit(solution)/shard_map/ppermute | solution.py:79
  72.4 19.4 %collective-permute-start.7 = (bf16[22,16,768]{2,1,0:T(8,128)(2,1)S(1)}, bf16[22,16,768]{2,1,0:T(8,128)(2,1)S(1)}, u32[]{:S(2)}, u32[]{:S(2)}) collective-permute-start(bf16[22,16,768]{2,1,0:T(8,128)(2,1)S(1)} %add_convert_fusion.5), channel_id=1, source_target_pairs={{0,12},{1,13},{2,14},{3,15},{4,0},{5,1},{6,2},{7,3},{8,4},{9,5},{1... | collective-permute-start | bytes 1622024 | tf_op jit(solution)/shard_map/ppermute | solution.py:79
  72.6 29.9 %collective-permute-start.1 = (bf16[22,16,768]{2,1,0:T(8,128)(2,1)S(1)}, bf16[22,16,768]{2,1,0:T(8,128)(2,1)S(1)}, u32[]{:S(2)}, u32[]{:S(2)}) collective-permute-start(bf16[22,16,768]{2,1,0:T(8,128)(2,1)S(1)} %get-tuple-element.40), channel_id=1, source_target_pairs={{0,12},{1,13},{2,14},{3,15},{4,0},{5,1},{6,2},{7,3},{8,4},{9,5},{1... | collective-permute-start | bytes 1622024 | tf_op jit(solution)/shard_map/ppermute | solution.py:79
  80.3 23.1 %collective-permute-start.3 = (bf16[22,16,768]{2,1,0:T(8,128)(2,1)S(1)}, bf16[22,16,768]{2,1,0:T(8,128)(2,1)S(1)}, u32[]{:S(2)}, u32[]{:S(2)}) collective-permute-start(bf16[22,16,768]{2,1,0:T(8,128)(2,1)S(1)} %add_convert_fusion.7), channel_id=1, source_target_pairs={{0,4},{1,5},{2,6},{3,7},{4,8},{5,9},{6,10},{7,11},{8,12},{9,13},{1... | collective-permute-start | bytes 1622024 | tf_op jit(solution)/shard_map/ppermute | solution.py:79
  82.8 24.0 %collective-permute-start.21 = (bf16[22,16,768]{2,1,0:T(8,128)(2,1)S(1)}, bf16[22,16,768]{2,1,0:T(8,128)(2,1)S(1)}, u32[]{:S(2)}, u32[]{:S(2)}) collective-permute-start(bf16[22,16,768]{2,1,0:T(8,128)(2,1)S(1)} %add_convert_fusion.3), channel_id=1, source_target_pairs={{0,4},{1,5},{2,6},{3,7},{4,8},{5,9},{6,10},{7,11},{8,12},{9,13},{1... | collective-permute-start | bytes 1622024 | tf_op jit(solution)/shard_map/ppermute | solution.py:79
  91.9 32.9 %collective-permute-start.26 = (bf16[22,16,768]{2,1,0:T(8,128)(2,1)S(1)}, bf16[22,16,768]{2,1,0:T(8,128)(2,1)S(1)}, u32[]{:S(2)}, u32[]{:S(2)}) collective-permute-start(bf16[22,16,768]{2,1,0:T(8,128)(2,1)S(1)} %add_convert_fusion), channel_id=1, source_target_pairs={{0,18},{1,19},{2,16},{3,17},{4,22},{5,23},{6,20},{7,21},{8,26},{9,... | collective-permute-start | bytes 1622024 | tf_op jit(solution)/shard_map/ppermute | solution.py:79
  102.5 14.8 %collective-permute-start.8 = (bf16[22,16,768]{2,1,0:T(8,128)(2,1)}, bf16[22,16,768]{2,1,0:T(8,128)(2,1)S(1)}, u32[]{:S(2)}, u32[]{:S(2)}) collective-permute-start(bf16[22,16,768]{2,1,0:T(8,128)(2,1)} %add_convert_fusion.4), channel_id=1, source_target_pairs={{0,18},{1,19},{2,16},{3,17},{4,22},{5,23},{6,20},{7,21},{8,26},{9,... | collective-permute-start | bytes 1622024 | tf_op jit(solution)/shard_map/ppermute | solution.py:79
  104.4 15.4 %collective-permute-start.4 = (bf16[22,16,768]{2,1,0:T(8,128)(2,1)}, bf16[22,16,768]{2,1,0:T(8,128)(2,1)S(1)}, u32[]{:S(2)}, u32[]{:S(2)}) collective-permute-start(bf16[22,16,768]{2,1,0:T(8,128)(2,1)} %add_convert_fusion.6), channel_id=1, source_target_pairs={{0,16},{1,17},{2,18},{3,19},{4,20},{5,21},{6,22},{7,23},{8,24},{9,... | collective-permute-start | bytes 1622024 | tf_op jit(solution)/shard_map/ppermute | solution.py:79
  107.8 21.4 %collective-permute-start.22 = (bf16[22,16,768]{2,1,0:T(8,128)(2,1)}, bf16[22,16,768]{2,1,0:T(8,128)(2,1)S(1)}, u32[]{:S(2)}, u32[]{:S(2)}) collective-permute-start(bf16[22,16,768]{2,1,0:T(8,128)(2,1)} %add_convert_fusion.2), channel_id=1, source_target_pairs={{0,16},{1,17},{2,18},{3,19},{4,20},{5,21},{6,22},{7,23},{8,24},{9,... | collective-permute-start | bytes 1622024 | tf_op jit(solution)/shard_map/ppermute | solution.py:79
  136.5 2.2 collective-permute-start.36
  138.7 11.2 %collective-permute-start.37 = (f32[208,384]{1,0:T(8,128)S(1)}, f32[208,384]{1,0:T(8,128)S(1)}, u32[]{:S(2)}, u32[]{:S(2)}) collective-permute-start(f32[208,384]{1,0:T(8,128)S(1)} %constant_dynamic-slice_fusion), channel_id=1, source_target_pairs={{0,64},{1,65},{2,66},{3,67},{4,68},{5,69},{6,70},{7,71},{8,72},{9,... | collective-permute-start | bytes 958472 | tf_op jit(solution)/shard_map/ppermute | solution.py:87
  150.0 5.4 %collective-permute-start.38 = (f32[104,384]{1,0:T(8,128)S(1)}, f32[104,384]{1,0:T(8,128)S(1)}, u32[]{:S(2)}, u32[]{:S(2)}) collective-permute-start(f32[104,384]{1,0:T(8,128)S(1)} %constant_dynamic-slice_fusion.2), channel_id=1, source_target_pairs={{0,32},{1,33},{2,34},{3,35},{4,36},{5,37},{6,38},{7,39},{8,40},{9,... | collective-permute-start | bytes 479240 | tf_op jit(solution)/shard_map/ppermute | solution.py:87
  155.4 5.4 %collective-permute-start.39 = (f32[104,384]{1,0:T(8,128)S(1)}, f32[104,384]{1,0:T(8,128)S(1)}, u32[]{:S(2)}, u32[]{:S(2)}) collective-permute-start(f32[104,384]{1,0:T(8,128)S(1)} %dynamic-slice_add_fusion.2), channel_id=1, source_target_pairs={{0,4},{1,5},{2,6},{3,7},{4,0},{5,1},{6,2},{7,3},{8,12},{9,13},{10,... | collective-permute-start | bytes 479240 | tf_op jit(solution)/shard_map/ppermute | solution.py:87
  156.2 24.8 %collective-permute-start.27 = (bf16[22,16,768]{2,1,0:T(8,128)(2,1)}, bf16[22,16,768]{2,1,0:T(8,128)(2,1)S(1)}, u32[]{:S(2)}, u32[]{:S(2)}) collective-permute-start(bf16[22,16,768]{2,1,0:T(8,128)(2,1)} %get-tuple-element.62), channel_id=1, source_target_pairs={{0,18},{1,19},{2,16},{3,17},{4,22},{5,23},{6,20},{7,21},{8,26},{9,... | collective-permute-start | bytes 1622024 | tf_op jit(solution)/shard_map/ppermute | solution.py:79
  156.7 26.7 %collective-permute-start.28 = (bf16[22,16,768]{2,1,0:T(8,128)(2,1)}, bf16[22,16,768]{2,1,0:T(8,128)(2,1)S(1)}, u32[]{:S(2)}, u32[]{:S(2)}) collective-permute-start(bf16[22,16,768]{2,1,0:T(8,128)(2,1)} %get-tuple-element.62), channel_id=1, source_target_pairs={{0,16},{1,17},{2,18},{3,19},{4,20},{5,21},{6,22},{7,23},{8,24},{9,... | collective-permute-start | bytes 1622024 | tf_op jit(solution)/shard_map/ppermute | solution.py:79
  160.8 7.2 %collective-permute-start.40 = (f32[104,384]{1,0:T(8,128)S(1)}, f32[104,384]{1,0:T(8,128)S(1)}, u32[]{:S(2)}, u32[]{:S(2)}) collective-permute-start(f32[104,384]{1,0:T(8,128)S(1)} %add.150), channel_id=1, source_target_pairs={{0,8},{1,9},{2,10},{3,11},{4,12},{5,13},{6,14},{7,15},{8,0},{9,1},... | collective-permute-start | bytes 479240 | tf_op jit(solution)/shard_map/ppermute | solution.py:87
  168.0 69.8 %copy-start.1 = (bf16[16,128,256]{2,1,0:T(8,128)(2,1)S(1)}, bf16[16,128,256]{2,1,0:T(8,128)(2,1)}, u32[]{:S(2)}) copy-start(bf16[16,128,256]{2,1,0:T(8,128)(2,1)} %constant.128.clone.own_t.beside_t) | copy-start | bytes 3145732
  168.0 5.4 %collective-permute-start.41 = (f32[104,384]{1,0:T(8,128)S(1)}, f32[104,384]{1,0:T(8,128)S(1)}, u32[]{:S(2)}, u32[]{:S(2)}) collective-permute-start(f32[104,384]{1,0:T(8,128)S(1)} %add.151), channel_id=1, source_target_pairs={{0,16},{1,17},{2,18},{3,19},{4,20},{5,21},{6,22},{7,23},{8,24},{9,... | collective-permute-start | bytes 479240 | tf_op jit(solution)/shard_map/ppermute | solution.py:87
  173.4 13.1 %collective-permute-start.42 = (f32[104,384]{1,0:T(8,128)S(1)}, f32[104,384]{1,0:T(8,128)S(1)}, u32[]{:S(2)}, u32[]{:S(2)}) collective-permute-start(f32[104,384]{1,0:T(8,128)S(1)} %add.152), channel_id=1, source_target_pairs={{0,2},{1,3},{2,0},{3,1},{4,6},{5,7},{6,4},{7,5},{8,10},{9,11},{10,... | collective-permute-start | bytes 479240 | tf_op jit(solution)/shard_map/ppermute | solution.py:87
  177.8 14.3 %collective-permute-start.9 = (bf16[22,16,768]{2,1,0:T(8,128)(2,1)}, bf16[22,16,768]{2,1,0:T(8,128)(2,1)}, u32[]{:S(2)}, u32[]{:S(2)}) collective-permute-start(bf16[22,16,768]{2,1,0:T(8,128)(2,1)} %get-tuple-element.47), channel_id=1, source_target_pairs={{0,18},{1,19},{2,16},{3,17},{4,22},{5,23},{6,20},{7,21},{8,26},{9,... | collective-permute-start | bytes 1622024 | tf_op jit(solution)/shard_map/ppermute | solution.py:79
  179.4 14.3 %collective-permute-start.10 = (bf16[22,16,768]{2,1,0:T(8,128)(2,1)}, bf16[22,16,768]{2,1,0:T(8,128)(2,1)}, u32[]{:S(2)}, u32[]{:S(2)}) collective-permute-start(bf16[22,16,768]{2,1,0:T(8,128)(2,1)} %get-tuple-element.47), channel_id=1, source_target_pairs={{0,16},{1,17},{2,18},{3,19},{4,20},{5,21},{6,22},{7,23},{8,24},{9,... | collective-permute-start | bytes 1622024 | tf_op jit(solution)/shard_map/ppermute | solution.py:79
  181.0 12.7 %collective-permute-start.31 = (bf16[22,16,768]{2,1,0:T(8,128)(2,1)S(1)}, bf16[22,16,768]{2,1,0:T(8,128)(2,1)S(1)}, u32[]{:S(2)}, u32[]{:S(2)}) collective-permute-start(bf16[22,16,768]{2,1,0:T(8,128)(2,1)S(1)} %collective-permute-done.27.rest_0_), channel_id=1, source_target_pairs={{0,4},{1,5},{2,6},{3,7},{4,8},{5,9},{6,10},{7,11},{8,12},{9,13},{1... | collective-permute-start | bytes 1622024 | tf_op jit(solution)/shard_map/ppermute | solution.py:79
  183.4 15.8 %collective-permute-start.30 = (bf16[22,16,768]{2,1,0:T(8,128)(2,1)S(1)}, bf16[22,16,768]{2,1,0:T(8,128)(2,1)S(1)}, u32[]{:S(2)}, u32[]{:S(2)}) collective-permute-start(bf16[22,16,768]{2,1,0:T(8,128)(2,1)S(1)} %collective-permute-done.28.rest_1_), channel_id=1, source_target_pairs={{0,12},{1,13},{2,14},{3,15},{4,0},{5,1},{6,2},{7,3},{8,4},{9,5},{1... | collective-permute-start | bytes 1622024 | tf_op jit(solution)/shard_map/ppermute | solution.py:79
  186.5 24.3 %collective-permute-start.29 = (bf16[22,16,768]{2,1,0:T(8,128)(2,1)S(1)}, bf16[22,16,768]{2,1,0:T(8,128)(2,1)S(1)}, u32[]{:S(2)}, u32[]{:S(2)}) collective-permute-start(bf16[22,16,768]{2,1,0:T(8,128)(2,1)S(1)} %collective-permute-done.27.rest_0_), channel_id=1, source_target_pairs={{0,12},{1,13},{2,14},{3,15},{4,0},{5,1},{6,2},{7,3},{8,4},{9,5},{1... | collective-permute-start | bytes 1622024 | tf_op jit(solution)/shard_map/ppermute | solution.py:79
  192.1 21.4 %collective-permute-start.43 = (f32[104,384]{1,0:T(8,128)S(1)}, f32[104,384]{1,0:T(8,128)S(1)}, u32[]{:S(2)}, u32[]{:S(2)}) collective-permute-start(f32[104,384]{1,0:T(8,128)S(1)} %add.153), channel_id=1, source_target_pairs={{0,32},{1,33},{2,34},{3,35},{4,36},{5,37},{6,38},{7,39},{8,40},{9,... | collective-permute-start | bytes 479240 | tf_op jit(solution)/shard_map/ppermute | solution.py:87
  193.7 22.5 %collective-permute-start.34 = (bf16[22,16,768]{2,1,0:T(8,128)(2,1)S(1)}, bf16[22,16,768]{2,1,0:T(8,128)(2,1)}, u32[]{:S(2)}, u32[]{:S(2)}) collective-permute-start(bf16[22,16,768]{2,1,0:T(8,128)(2,1)S(1)} %collective-permute-done.28.rest_1_), channel_id=1, source_target_pairs={{0,4},{1,5},{2,6},{3,7},{4,8},{5,9},{6,10},{7,11},{8,12},{9,13},{1... | collective-permute-start | bytes 1622024 | tf_op jit(solution)/shard_map/ppermute | solution.py:79
  193.8 28.0 %collective-permute-start.13 = (bf16[22,16,768]{2,1,0:T(8,128)(2,1)}, bf16[22,16,768]{2,1,0:T(8,128)(2,1)}, u32[]{:S(2)}, u32[]{:S(2)}) collective-permute-start(bf16[22,16,768]{2,1,0:T(8,128)(2,1)} %collective-permute-done.9.rest_0_), channel_id=1, source_target_pairs={{0,4},{1,5},{2,6},{3,7},{4,8},{5,9},{6,10},{7,11},{8,12},{9,13},{1... | collective-permute-start | bytes 1622024 | tf_op jit(solution)/shard_map/ppermute | solution.py:79
  199.2 23.3 %collective-permute-start.12 = (bf16[22,16,768]{2,1,0:T(8,128)(2,1)}, bf16[22,16,768]{2,1,0:T(8,128)(2,1)}, u32[]{:S(2)}, u32[]{:S(2)}) collective-permute-start(bf16[22,16,768]{2,1,0:T(8,128)(2,1)} %collective-permute-done.10.rest_1_), channel_id=1, source_target_pairs={{0,12},{1,13},{2,14},{3,15},{4,0},{5,1},{6,2},{7,3},{8,4},{9,5},{1... | collective-permute-start | bytes 1622024 | tf_op jit(solution)/shard_map/ppermute | solution.py:79
  211.6 21.8 %collective-permute-start.32 = (bf16[22,16,768]{2,1,0:T(8,128)(2,1)S(1)}, bf16[22,16,768]{2,1,0:T(8,128)(2,1)}, u32[]{:S(2)}, u32[]{:S(2)}) collective-permute-start(bf16[22,16,768]{2,1,0:T(8,128)(2,1)S(1)} %collective-permute-done.31.rest_6_), channel_id=1, source_target_pairs={{0,4},{1,5},{2,6},{3,7},{4,8},{5,9},{6,10},{7,11},{8,12},{9,13},{1... | collective-permute-start | bytes 1622024 | tf_op jit(solution)/shard_map/ppermute | solution.py:79
  213.5 20.5 %collective-permute-start.33 = (bf16[22,16,768]{2,1,0:T(8,128)(2,1)S(1)}, bf16[22,16,768]{2,1,0:T(8,128)(2,1)}, u32[]{:S(2)}, u32[]{:S(2)}) collective-permute-start(bf16[22,16,768]{2,1,0:T(8,128)(2,1)S(1)} %collective-permute-done.30.rest_3_), channel_id=1, source_target_pairs={{0,12},{1,13},{2,14},{3,15},{4,0},{5,1},{6,2},{7,3},{8,4},{9,5},{1... | collective-permute-start | bytes 1622024 | tf_op jit(solution)/shard_map/ppermute | solution.py:79
  215.4 18.6 %copy-start.21 = (f32[104,384]{1,0:T(8,128)}, f32[104,384]{1,0:T(8,128)S(1)}, u32[]{:S(2)}) copy-start(f32[104,384]{1,0:T(8,128)S(1)} %get-tuple-element.75) | copy-start | bytes 479236
  216.2 28.8 %collective-permute-start.44 = (f32[208,384]{1,0:T(8,128)}, f32[208,384]{1,0:T(8,128)S(1)}, u32[]{:S(2)}, u32[]{:S(2)}) collective-permute-start(f32[208,384]{1,0:T(8,128)} %pad_maximum_fusion.2), channel_id=1, source_target_pairs={{0,64},{1,65},{2,66},{3,67},{4,68},{5,69},{6,70},{7,71},{8,72},{9,... | collective-permute-start | bytes 958472 | tf_op jit(solution)/shard_map/ppermute | solution.py:87
  221.8 26.6 %collective-permute-start.11 = (bf16[22,16,768]{2,1,0:T(8,128)(2,1)}, bf16[22,16,768]{2,1,0:T(8,128)(2,1)}, u32[]{:S(2)}, u32[]{:S(2)}) collective-permute-start(bf16[22,16,768]{2,1,0:T(8,128)(2,1)} %collective-permute-done.9.rest_0_), channel_id=1, source_target_pairs={{0,12},{1,13},{2,14},{3,15},{4,0},{5,1},{6,2},{7,3},{8,4},{9,5},{1... | collective-permute-start | bytes 1622024 | tf_op jit(solution)/shard_map/ppermute | solution.py:79
  222.6 26.3 %collective-permute-start.16 = (bf16[22,16,768]{2,1,0:T(8,128)(2,1)}, bf16[22,16,768]{2,1,0:T(8,128)(2,1)}, u32[]{:S(2)}, u32[]{:S(2)}) collective-permute-start(bf16[22,16,768]{2,1,0:T(8,128)(2,1)} %collective-permute-done.10.rest_1_), channel_id=1, source_target_pairs={{0,4},{1,5},{2,6},{3,7},{4,8},{5,9},{6,10},{7,11},{8,12},{9,13},{1... | collective-permute-start | bytes 1622024 | tf_op jit(solution)/shard_map/ppermute | solution.py:79
  233.4 19.5 %collective-permute-start.14 = (bf16[22,16,768]{2,1,0:T(8,128)(2,1)}, bf16[22,16,768]{2,1,0:T(8,128)(2,1)}, u32[]{:S(2)}, u32[]{:S(2)}) collective-permute-start(bf16[22,16,768]{2,1,0:T(8,128)(2,1)} %collective-permute-done.13.rest_6_), channel_id=1, source_target_pairs={{0,4},{1,5},{2,6},{3,7},{4,8},{5,9},{6,10},{7,11},{8,12},{9,13},{1... | collective-permute-start | bytes 1622024 | tf_op jit(solution)/shard_map/ppermute | solution.py:79
  234.0 18.9 %collective-permute-start.15 = (bf16[22,16,768]{2,1,0:T(8,128)(2,1)}, bf16[22,16,768]{2,1,0:T(8,128)(2,1)}, u32[]{:S(2)}, u32[]{:S(2)}) collective-permute-start(bf16[22,16,768]{2,1,0:T(8,128)(2,1)} %collective-permute-done.12.rest_3_), channel_id=1, source_target_pairs={{0,12},{1,13},{2,14},{3,15},{4,0},{5,1},{6,2},{7,3},{8,4},{9,5},{1... | collective-permute-start | bytes 1622024 | tf_op jit(solution)/shard_map/ppermute | solution.py:79
  245.7 26.5 %collective-permute-start.35 = (bf16[8,11,16,768]{3,2,1,0:T(8,128)(2,1)}, bf16[8,11,16,768]{3,2,1,0:T(8,128)(2,1)S(1)}, u32[]{:S(2)}, u32[]{:S(2)}) collective-permute-start(bf16[8,11,16,768]{3,2,1,0:T(8,128)(2,1)} %get-tuple-element.64), channel_id=1, source_target_pairs={{0,1},{1,0},{2,3},{3,2},{4,5},{5,4},{6,7},{7,6},{8,9},{9,8},{10,11... | collective-permute-start | bytes 6488072 | tf_op jit(solution)/shard_map/ppermute | solution.py:87
  248.3 11.7 %collective-permute-start.45 = (f32[416,384]{1,0:T(8,128)}, f32[416,384]{1,0:T(8,128)}, u32[]{:S(2)}, u32[]{:S(2)}) collective-permute-start(f32[416,384]{1,0:T(8,128)} %pad_maximum_fusion.1), channel_id=1, source_target_pairs={{0,1},{1,0},{2,3},{3,2},{4,5},{5,4},{6,7},{7,6},{8,9},{9,8},{10,11... | collective-permute-start | bytes 1916936 | tf_op jit(solution)/shard_map/ppermute | solution.py:87
  260.1 23.5 %collective-permute-start.17 = (bf16[8,11,16,768]{3,2,1,0:T(8,128)(2,1)}, bf16[8,11,16,768]{3,2,1,0:T(8,128)(2,1)}, u32[]{:S(2)}, u32[]{:S(2)}) collective-permute-start(bf16[8,11,16,768]{3,2,1,0:T(8,128)(2,1)} %get-tuple-element.49), channel_id=1, source_target_pairs={{0,1},{1,0},{2,3},{3,2},{4,5},{5,4},{6,7},{7,6},{8,9},{9,8},{10,11... | collective-permute-start | bytes 6488072 | tf_op jit(solution)/shard_map/ppermute | solution.py:87
  (25 other events, 119.9 us)
